TPU v7x, 32 devices: a whole 2x2x4 slice. The times are simulated.
32 devices in a mesh: shots: 2 (over x), xline: 8 (over z, y), inline: 2 (over core).
Axes of the slice: x: 2, y: 2, z: 4, core: 2. Of those that a mesh axis runs over, the one named last changes fastest.
Arguments:
- fwd_now: float32 [128, 64, 256], P(('shots', 'inline'), 'xline'), parts along dimension 0, may hold values from -6 to 6
- fwd_before: float32 [128, 64, 256], P(('shots', 'inline'), 'xline'), parts along dimension 0, may hold values from -6 to 6
- adj_now: float32 [128, 64, 256], P(('shots', 'inline'), 'xline'), parts along dimension 0, may hold values from -6 to 6
- adj_before: float32 [128, 64, 256], P(('shots', 'inline'), 'xline'), parts along dimension 0, may hold values from -6 to 6
- velocity: float32 [64, 64, 256], P('inline', 'xline'), may hold values from 0.2 to 0.4
- log_density: float32 [64, 64, 256], P('inline', 'xline'), may hold values from -0.3 to 0.3
- observed: float32 [16, 2048], P('shots', ('xline', 'inline')), parts along dimension 0, may hold values from -48 to 48
- rec_cells: int32 [16, 128], P(('xline', 'inline')), may hold values from 0 to 65535
- rec_counts: int32 [16, 16], P(('xline', 'inline')), may hold values from 0 to 8, as said below
- src_cell: int32 [32], P('shots'), parts along dimension 0, may hold values from 0 to 1048575
- wavelet: float32 [16, 16], P('shots'), parts along dimension 0, may hold values from -144 to 144
Outputs:
- gradient: float32 [512, 64, 64], P(('shots', 'xline'), 'inline'), parts along dimension 0
- adjoint_state: float32 [128, 64, 256], P(('shots', 'inline'), 'xline'), parts along dimension 0
- adjoint_previous: float32 [128, 64, 256], P(('shots', 'inline'), 'xline'), parts along dimension 0
There are 2 independent parts, one for each index of `shots`. A program takes and returns all parts, laid end to end along the dimension named above; an argument that names none is the same for every part. Nothing has to cross between parts.
Inputs may be any that keep to these rules, and one draw needn't show every extreme that they name: rec_counts[o, s] live slots of the 8 that device s sends to subdomain o; in every draw one subdomain receives 8 live slots from every device.
All inputs are finite; a program needn't handle non-finite values.
Results may differ from a plain program's by a relative error of at most 0.04.
Values sent between devices are 32-bit elements; how exact they have to be, the bound alone decides.
A program may use at most 64 MiB of HBM per device.

v0:
```python
import functools

import jax
import jax.numpy as jnp
from jax import lax
from jax.experimental import pallas as pl
from jax.experimental.pallas import tpu as pltpu
from jax.sharding import PartitionSpec as P

CAP = 8
SMOOTH = 16
MESH = pl.DeviceIdType.MESH

SECOND_COEFFS = (-205.0 / 72.0, 8.0 / 5.0, -1.0 / 5.0, 8.0 / 315.0, -1.0 / 560.0)
FIRST_COEFFS = (4.0 / 5.0, -1.0 / 5.0, 4.0 / 105.0, -1.0 / 280.0)
LEFT, RIGHT, UP, DOWN = 0, 1, 2, 3
DENSITY = 4


def split_bf16(value):
    high = value.astype(jnp.bfloat16)
    low = (value - high.astype(jnp.float32)).astype(jnp.bfloat16)
    return high, low


def dot(a, b):
    return jnp.dot(a, b, preferred_element_type=jnp.float32)


def wave_kernel(
    sizes,
    fwd_now, fwd_before, adj_now, adj_before, velocity, density,
    traces, rec_row, rec_row_t, rec_z, rec_live, src_row, src_z, wavelet,
    raw_out, last_out, previous_out,
    field, x_in, x_out, accel, base, image, slopes, speed_sq,
    row_map, row_map_t, z_map, z_high, z_low, residual_ref,
    send_sem, recv_sem,
):
    n_i, n_x, depth, steps, n_xline, n_inline = sizes
    rows = n_i * n_x
    xl = lax.axis_index("xline")
    core = lax.axis_index("inline")
    side = lax.rem(xl, 2)
    half = lax.rem(side + lax.rem(core, 2), 2)
    mate = xl + 1 - 2 * side
    has = (
        xl >= 2,
        xl < n_xline - 2,
        core * 2 + half > 0,
        core * 2 + half < 2 * n_inline - 1,
    )
    target = (
        {"xline": xl - 2},
        {"xline": xl + 2},
        {"xline": jnp.where(half == 1, mate, xl), "inline": jnp.where(half == 1, core, core - 1)},
        {"xline": jnp.where(half == 0, mate, xl), "inline": jnp.where(half == 0, core, core + 1)},
    )
    inner_x = pl.ds(8, n_x)

    middle = n_i // 2

    def copy_of(idx, way, part):
        part_rows = pl.ds(part * middle, middle)
        sem = way
        if way == LEFT:
            src, dst = x_out.at[idx, 0, part_rows], x_in.at[idx, 1, part_rows]
            sem = way + 4 * part
        elif way == RIGHT:
            src, dst = x_out.at[idx, 1, part_rows], x_in.at[idx, 0, part_rows]
            sem = way + 4 * part
        elif way == UP:
            src = field.at[idx, pl.ds(4, 4), inner_x, :]
            dst = field.at[idx, pl.ds(n_i + 4, 4), inner_x, :]
        else:
            src = field.at[idx, pl.ds(n_i, 4), inner_x, :]
            dst = field.at[idx, pl.ds(0, 4), inner_x, :]
        return pltpu.make_async_remote_copy(
            src_ref=src, dst_ref=dst,
            send_sem=send_sem.at[idx, sem], recv_sem=recv_sem.at[idx, sem],
            device_id=target[way], device_id_type=MESH,
        )

    def send(idx, part):
        part_rows = pl.ds(part * middle, middle)
        field_rows = pl.ds(4 + part * middle, middle)
        x_out[idx, 0, part_rows] = field[idx, field_rows, pl.ds(8, 4), :]
        x_out[idx, 1, part_rows] = field[idx, field_rows, pl.ds(4 + n_x, 4), :]
        for way in (LEFT, RIGHT, UP + part):
            @pl.when(has[way])
            def _():
                copy_of(idx, way, part).start()

    def finish(idx, part):
        for way in (LEFT, RIGHT, UP + part):
            @pl.when(has[way])
            def _():
                copy_of(idx, way, part).wait_send()
                copy_of(idx, way ^ 1, part).wait_recv()
        part_rows = pl.ds(part * middle, middle)
        field_rows = pl.ds(4 + part * middle, middle)
        field[idx, field_rows, pl.ds(4, 4), :] = x_in[idx, 0, part_rows]
        field[idx, field_rows, pl.ds(8 + n_x, 4), :] = x_in[idx, 1, part_rows]

    for idx in range(5):
        field[idx, pl.ds(0, 4)] = jnp.zeros((4,) + field.shape[2:], jnp.float32)
        field[idx, pl.ds(n_i + 4, 4)] = jnp.zeros((4,) + field.shape[2:], jnp.float32)
    x_in[...] = jnp.zeros(x_in.shape, jnp.float32)

    barrier = pltpu.get_barrier_semaphore()
    for way in range(4):
        @pl.when(has[way])
        def _():
            pl.semaphore_signal(barrier, inc=1, device_id=target[way], device_id_type=MESH)
    pl.semaphore_wait(barrier, sum(present.astype(jnp.int32) for present in has))

    inner_i = pl.ds(4, n_i)
    field[DENSITY, inner_i, inner_x, :] = density[...]
    field[0, inner_i, inner_x, :] = fwd_now[...]
    send(DENSITY, 0)
    send(DENSITY, 1)
    send(0, 0)
    send(0, 1)
    field[2, inner_i, inner_x, :] = adj_now[...]
    send(2, 0)
    send(2, 1)
    field[1, inner_i, inner_x, :] = fwd_before[...]
    field[3, inner_i, inner_x, :] = adj_before[...]

    speed_sq[...] = velocity[...] * velocity[...]
    image[...] = jnp.zeros(image.shape, jnp.float32)
    slots = rec_row.shape[0]
    row_map[...] = (lax.broadcasted_iota(jnp.int32, (rows, slots), 0) == rec_row_t[...]).astype(jnp.float32).astype(jnp.bfloat16)
    row_map_t[...] = (lax.broadcasted_iota(jnp.int32, (slots, rows), 1) == rec_row[...]).astype(jnp.float32).astype(jnp.bfloat16)
    z_map[...] = (lax.broadcasted_iota(jnp.int32, (slots, depth), 1) == rec_z[...]).astype(jnp.float32)
    src_rows = (lax.broadcasted_iota(jnp.int32, (rows, src_row.shape[1]), 0) == src_row[...]).astype(jnp.float32)
    src_cols = (lax.broadcasted_iota(jnp.int32, (src_z.shape[0], depth), 1) == src_z[...]).astype(jnp.float32).astype(jnp.bfloat16)
    offset = lax.broadcasted_iota(jnp.int32, (depth, depth), 0) - lax.broadcasted_iota(jnp.int32, (depth, depth), 1)
    second = jnp.where(offset == 0, 3.0 * SECOND_COEFFS[0], 0.0)
    first = jnp.zeros((depth, depth), jnp.float32)
    for k in range(1, 5):
        second = jnp.where((offset == k) | (offset == -k), SECOND_COEFFS[k], second)
        first = jnp.where(offset == k, FIRST_COEFFS[k - 1], first)
        first = jnp.where(offset == -k, -FIRST_COEFFS[k - 1], first)
    high, low = split_bf16(second)
    z_high[:, pl.ds(0, depth)] = high
    z_low[:, pl.ds(0, depth)] = low
    high, low = split_bf16(first)
    z_high[:, pl.ds(depth, depth)] = high
    z_low[:, pl.ds(depth, depth)] = low

    def flat(idx):
        return field[idx, inner_i, inner_x, :].reshape(rows, depth)

    def along_depth(idx):
        high, low = split_bf16(flat(idx))
        both = dot(high, z_high[...]) + (dot(low, z_high[...]) + dot(high, z_low[...]))
        return both[:, :depth], both[:, depth:]

    def across(idx, i):
        lap = slope_i = slope_x = None
        for k in range(1, 5):
            plus_i = field[idx, i + 4 + k, inner_x, :]
            minus_i = field[idx, i + 4 - k, inner_x, :]
            plus_x = field[idx, i + 4, pl.ds(8 + k, n_x), :]
            minus_x = field[idx, i + 4, pl.ds(8 - k, n_x), :]
            terms = (
                SECOND_COEFFS[k] * ((plus_i + minus_i) + (plus_x + minus_x)),
                FIRST_COEFFS[k - 1] * (plus_i - minus_i),
                FIRST_COEFFS[k - 1] * (plus_x - minus_x),
            )
            if lap is None:
                lap, slope_i, slope_x = terms
            else:
                lap, slope_i, slope_x = lap + terms[0], slope_i + terms[1], slope_x + terms[2]
        return lap, slope_i, slope_x

    def prepare(idx, term):
        lap, slope = along_depth(idx)
        partial = term + speed_sq[...].reshape(rows, depth) * (lap - slopes[2].reshape(rows, depth) * slope)
        base[...] = partial.reshape(n_i, n_x, depth)

    slopes[2] = along_depth(DENSITY)[1].reshape(n_i, n_x, depth)
    finish(DENSITY, 0)
    finish(DENSITY, 1)

    @pl.loop(0, n_i)
    def _(i):
        _, slope_i, slope_x = across(DENSITY, i)
        slopes[0, i] = slope_i
        slopes[1, i] = slope_x

    @pl.loop(0, steps)
    def _(t):
        now = lax.rem(t, 2)
        other = 1 - now
        high, low = split_bf16(src_rows * wavelet[pl.ds(t, 1), :])
        prepare(now, dot(high, src_cols) + dot(low, src_cols))

        for part in range(2):
            finish(now, part)

            @pl.loop(part * middle, (part + 1) * middle)
            def _(i):
                lap, slope_i, slope_x = across(now, i)
                change = base[i] + speed_sq[i] * (lap - slopes[0, i] * slope_i - slopes[1, i] * slope_x)
                accel[t, i] = change
                field[other, i + 4, inner_x, :] = (
                    2.0 * field[now, i + 4, inner_x, :] - field[other, i + 4, inner_x, :] + change
                )

            @pl.when(t < steps - 1)
            def _():
                send(other, part)

        high, low = split_bf16(flat(other))
        picked = dot(row_map_t[...], high) + dot(row_map_t[...], low)
        predicted = jnp.sum(picked * z_map[...], axis=1, keepdims=True)
        column = lax.broadcasted_iota(jnp.int32, traces.shape, 1) == t
        seen = jnp.sum(jnp.where(column, traces[...], 0.0), axis=1, keepdims=True)
        residual_ref[t] = rec_live[...] * (predicted - seen)

    @pl.loop(0, steps)
    def _(j):
        now = 2 + lax.rem(j, 2)
        other = 5 - now
        t = steps - 1 - j
        high, low = split_bf16(residual_ref[t] * z_map[...])
        prepare(now, dot(row_map[...], high) + dot(row_map[...], low))

        for part in range(2):
            finish(now, part)

            @pl.loop(part * middle, (part + 1) * middle)
            def _(i):
                lap, slope_i, slope_x = across(now, i)
                change = base[i] + speed_sq[i] * (lap - slopes[0, i] * slope_i - slopes[1, i] * slope_x)
                fresh = 2.0 * field[now, i + 4, inner_x, :] - field[other, i + 4, inner_x, :] + change
                field[other, i + 4, inner_x, :] = fresh
                image[i] += fresh * accel[t, i]

            @pl.when(j < steps - 1)
            def _():
                send(other, part)

    raw_out[...] = image[...] * (2.0 / steps) / velocity[...]
    last_out[...] = field[2 + steps % 2, inner_i, inner_x, :]
    previous_out[...] = field[2 + (steps - 1) % 2, inner_i, inner_x, :]


def per_device(
    fwd_now, fwd_before, adj_now, adj_before, velocity, log_density,
    observed, rec_cells, rec_counts, src_cell, wavelet,
):
    tile_i, tile_x, depth = fwd_now.shape
    steps = wavelet.shape[0]
    n_xline = lax.axis_size("xline")
    n_inline = lax.axis_size("inline")
    full_x = tile_x * n_xline
    n_i, n_x = tile_i // 2, tile_x * 2
    xl = lax.axis_index("xline")
    core = lax.axis_index("inline")
    side = xl % 2
    half = (side + core) % 2
    swap = [(k, k ^ 1) for k in range(n_xline)]

    def pair_up(mine, theirs, axis):
        return jnp.where(
            side == 0,
            jnp.concatenate([mine, theirs], axis=axis),
            jnp.concatenate([theirs, mine], axis=axis),
        )

    def gather_pair(value):
        kept = lax.dynamic_slice_in_dim(value, half * n_i, n_i, axis=0)
        sent = lax.dynamic_slice_in_dim(value, (1 - half) * n_i, n_i, axis=0)
        return pair_up(kept, lax.ppermute(sent, "xline", swap), 1)

    columns = observed.reshape(steps, n_xline // 2, 1, 2, n_inline, CAP).swapaxes(3, 4)
    columns = jnp.broadcast_to(columns, (steps, n_xline // 2, 2, n_inline, 2, CAP))
    routed = lax.all_to_all(
        columns.reshape(steps, -1), ("xline", "inline"), split_axis=1, concat_axis=1, tiled=True
    )
    live = (jnp.arange(CAP)[None, :] < rec_counts[0][:, None]).astype(jnp.int32).reshape(1, -1)
    lists = jnp.concatenate([rec_cells, live], axis=0)
    lists = pair_up(lists, lax.ppermute(lists, "xline", swap), 1)
    traces = routed.reshape(steps, -1, 2, CAP).transpose(2, 1, 3, 0).reshape(-1, steps)
    cells = lists[0]
    slots = cells.shape[0]
    cell_i = cells // (tile_x * depth) - half * n_i
    cell_x = cells // depth % tile_x + jnp.where(jnp.arange(slots) < slots // 2, 0, tile_x)
    rec_row = jnp.where((cell_i >= 0) & (cell_i < n_i), cell_i * n_x + cell_x, -1)
    rec_z = cells % depth
    src_i = src_cell // (full_x * depth) - (core * tile_i + half * n_i)
    src_x = src_cell // depth % full_x - (xl // 2) * n_x
    inside = (src_i >= 0) & (src_i < n_i) & (src_x >= 0) & (src_x < n_x)
    src_row = jnp.where(inside, src_i * n_x + src_x, -1)
    src_z = src_cell % depth

    block = (n_i, n_x, depth)
    rows = n_i * n_x
    vmem = pl.BlockSpec(memory_space=pltpu.VMEM)
    kernel = functools.partial(wave_kernel, (n_i, n_x, depth, steps, n_xline, n_inline))
    raw, last, previous = pl.pallas_call(
        kernel,
        out_shape=[jax.ShapeDtypeStruct(block, jnp.float32)] * 3,
        in_specs=[vmem] * 14,
        out_specs=[vmem] * 3,
        scratch_shapes=[
            pltpu.VMEM((5, n_i + 8, n_x + 16, depth), jnp.float32),
            pltpu.VMEM((5, 2, n_i, 4, depth), jnp.float32),
            pltpu.VMEM((5, 2, n_i, 4, depth), jnp.float32),
            pltpu.VMEM((steps,) + block, jnp.float32),
            pltpu.VMEM(block, jnp.float32),
            pltpu.VMEM(block, jnp.float32),
            pltpu.VMEM((3,) + block, jnp.float32),
            pltpu.VMEM(block, jnp.float32),
            pltpu.VMEM((rows, slots), jnp.bfloat16),
            pltpu.VMEM((slots, rows), jnp.bfloat16),
            pltpu.VMEM((slots, depth), jnp.float32),
            pltpu.VMEM((depth, 2 * depth), jnp.bfloat16),
            pltpu.VMEM((depth, 2 * depth), jnp.bfloat16),
            pltpu.VMEM((steps, slots, 1), jnp.float32),
            pltpu.SemaphoreType.DMA((5, 6)),
            pltpu.SemaphoreType.DMA((5, 6)),
        ],
        compiler_params=pltpu.CompilerParams(
            collective_id=0, has_side_effects=True, vmem_limit_bytes=56 * 1024 * 1024
        ),
    )(
        gather_pair(fwd_now), gather_pair(fwd_before), gather_pair(adj_now), gather_pair(adj_before),
        gather_pair(velocity), gather_pair(log_density),
        traces, rec_row[:, None], rec_row[None, :], rec_z[:, None],
        lists[1].astype(jnp.float32)[:, None], src_row[None, :], src_z[:, None], wavelet,
    )

    def split_pair(value):
        kept = lax.dynamic_slice_in_dim(value, side * tile_x, tile_x, axis=1)
        sent = lax.dynamic_slice_in_dim(value, (1 - side) * tile_x, tile_x, axis=1)
        got = lax.ppermute(sent, "xline", swap)
        return jnp.where(
            half == 0, jnp.concatenate([kept, got], axis=0), jnp.concatenate([got, kept], axis=0)
        )

    pieces = n_xline
    columns = lax.all_to_all(
        raw.reshape(n_i, n_x, pieces, depth // pieces).transpose(2, 0, 1, 3),
        "xline", split_axis=0, concat_axis=0, tiled=True,
    ).reshape(n_xline // 2, 2, n_i, n_x, depth // pieces)
    columns = jnp.where(core % 2 == 0, columns, columns[:, ::-1])
    positions = jnp.arange(full_x).astype(jnp.float32)
    weights = jnp.exp(-jnp.abs(positions[:, None] - positions[None, :]) / SMOOTH)
    weights = weights / jnp.sum(weights, axis=1, keepdims=True)
    gradient = jnp.einsum(
        "phixz,ypx->zhiy", columns, weights.reshape(full_x, n_xline // 2, n_x),
        precision=lax.Precision.HIGHEST,
    ).reshape(depth // pieces, tile_i, full_x)
    return gradient, split_pair(last), split_pair(previous)


def solution(mesh):
    return jax.shard_map(
        per_device,
        mesh=mesh,
        in_specs=(
            P(("shots", "inline"), "xline", None),
            P(("shots", "inline"), "xline", None),
            P(("shots", "inline"), "xline", None),
            P(("shots", "inline"), "xline", None),
            P("inline", "xline", None),
            P("inline", "xline", None),
            P("shots", ("xline", "inline")),
            P(("xline", "inline"), None),
            P(("xline", "inline"), None),
            P("shots"),
            P("shots", None),
        ),
        out_specs=(
            P(("shots", "xline"), "inline", None),
            P(("shots", "inline"), "xline", None),
            P(("shots", "inline"), "xline", None),
        ),
        check_vma=False,
    )
```

profile of v0, /device:TPU:0, one launch (start us, length us, event | category | flops | bytes accessed | tf_op | source)
XLA Modules:
  0.0 118.0 jit_solution(9975428116013233697)
XLA Ops:
  0.7 1.0 constant_dynamic-slice_fusion.13
  1.7 3.0 %collective-permute-start.1 = (f32[16,8,256]{2,1,0:T(8,128)S(1)}, f32[16,8,256]{2,1,0:T(8,128)S(1)}, u32[]{:S(2)}, u32[]{:S(2)}) collective-permute-start(f32[16,8,256]{2,1,0:T(8,128)S(1)} %get-tuple-element.37), channel_id=1, source_target_pairs={{0,2},{2,0},{4,6},{6,4},{8,10},{10,8},{12,14},{14,12},{1,3},{3,1},... | collective-permute-start | bytes 393224 | tf_op jit(solution)/shard_map/ppermute | solution.py:276
  4.9 2.1 %collective-permute-start.3 = (f32[16,8,256]{2,1,0:T(8,128)S(1)}, f32[16,8,256]{2,1,0:T(8,128)S(1)}, u32[]{:S(2)}, u32[]{:S(2)}) collective-permute-start(f32[16,8,256]{2,1,0:T(8,128)S(1)} %get-tuple-element.33), channel_id=1, source_target_pairs={{0,2},{2,0},{4,6},{6,4},{8,10},{10,8},{12,14},{14,12},{1,3},{3,1},... | collective-permute-start | bytes 393224 | tf_op jit(solution)/shard_map/ppermute | solution.py:276
  7.0 0.1 collective-permute-start.4
  7.1 0.5 copy-done.9
  7.8 0.6 copy-done.8
  8.4 1.4 %collective-permute-start.6 = (s32[2,128]{1,0:T(2,128)S(1)}, s32[2,128]{1,0:T(2,128)S(1)}, u32[]{:S(2)}, u32[]{:S(2)}) collective-permute-start(s32[2,128]{1,0:T(2,128)S(1)} %pad_add_fusion), channel_id=1, source_target_pairs={{0,2},{2,0},{4,6},{6,4},{8,10},{10,8},{12,14},{14,12},{1,3},{3,1},... | collective-permute-start | bytes 3080 | tf_op jit(solution)/shard_map/ppermute | solution.py:285
  9.9 0.1 reshape.304
  10.1 0.1 all_to_all.9
  10.3 0.7 reshape.313
  10.9 5.0 %all-to-all-start = ((f32[16,1,128]{2,1,0:T(1,128)}), f32[16,1,128]{2,1,0:T(1,128)S(1)}, u32[]{:S(2)}, u32[]{:S(2)}) async-start(f32[16,1,128]{2,1,0:T(1,128)} %reshape.313), calls=%async_computation | async-start | bytes 16384 | tf_op jit(solution)/shard_map/all_to_all | solution.py:280
  16.0 0.9 copy-done.5
  17.0 0.6 copy-done.10
  17.6 0.6 fusion.26
  18.2 0.2 exponential_reduce_fusion
  18.4 0.7 copy.62.src_z
  19.1 1.9 %collective-permute-start.5 = (f32[16,8,256]{2,1,0:T(8,128)S(1)}, f32[16,8,256]{2,1,0:T(8,128)S(1)}, u32[]{:S(2)}, u32[]{:S(2)}) collective-permute-start(f32[16,8,256]{2,1,0:T(8,128)S(1)} %get-tuple-element.29), channel_id=1, source_target_pairs={{0,2},{2,0},{4,6},{6,4},{8,10},{10,8},{12,14},{14,12},{1,3},{3,1},... | collective-permute-start | bytes 393224 | tf_op jit(solution)/shard_map/ppermute | solution.py:276
  21.0 0.6 fusion.24
  21.6 0.1 copy.57
  21.8 1.0 add_select_fusion
  22.7 0.8 copy.61.rec_live
  23.5 0.5 broadcast.347
  24.0 0.6 reduce
  24.8 0.8 copy.56
  25.6 0.1 collective-permute-start
  25.7 0.7 maximum_select_fusion.1.fwd_before
  26.4 0.7 maximum_select_fusion.2.adj_now
  27.1 0.7 maximum_select_fusion.3.adj_before
  27.9 0.7 maximum_select_fusion.4.velocity
  28.6 0.7 maximum_select_fusion.5.density
  29.3 1.5 %collective-permute-done = f32[16,8,256]{2,1,0:T(8,128)S(1)} collective-permute-done((f32[16,8,256]{2,1,0:T(8,128)S(1)}, f32[16,8,256]{2,1,0:T(8,128)S(1)}, u32[]{:S(2)}, u32[]{:S(2)}) %collective-permute-start) | collective-permute-done | bytes 131104 | tf_op jit(solution)/shard_map/ppermute | solution.py:276
  30.8 0.7 maximum_select_fusion.fwd_now
  31.6 65.4 %shard_map.130 = (f32[16,16,256]{2,1,0:T(8,128)}, f32[16,16,256]{2,1,0:T(8,128)}, f32[16,16,256]{2,1,0:T(8,128)}) custom-call(f32[16,16,256]{2,1,0:T(8,128)} %maximum_select_fusion.fwd_now, f32[16,16,256]{2,1,0:T(8,128)} %maximum_select_fusion.1.fwd_before, f32[16,16,256]{2,1,0:T(8,128)} %maximum_select_fusion.2.adj_now, ...), custom_call_target="tpu_custom_call" | custom-call | tf_op jit(solution)/shard_map/pallas_call | solution.py:303
  97.0 1.0 constant_dynamic-slice_fusion.1
  98.0 1.9 %collective-permute-start.8 = (f32[16,8,256]{2,1,0:T(8,128)S(1)}, f32[16,8,256]{2,1,0:T(8,128)S(1)}, u32[]{:S(2)}, u32[]{:S(2)}) collective-permute-start(f32[16,8,256]{2,1,0:T(8,128)S(1)} %get-tuple-element.25), channel_id=1, source_target_pairs={{0,2},{2,0},{4,6},{6,4},{8,10},{10,8},{12,14},{14,12},{1,3},{3,1},... | collective-permute-start | bytes 393224 | tf_op jit(solution)/shard_map/ppermute | solution.py:339
  100.0 0.3 reshape.307
  100.2 0.2 copy.70
  100.4 1.2 reshape.315
  101.6 3.6 %all-to-all-start.1 = ((f32[8,1,8192]{2,1,0:T(1,128)}), f32[8,1,8192]{2,1,0:T(1,128)S(1)}, u32[]{:S(2)}, u32[]{:S(2)}) async-start(f32[8,1,8192]{2,1,0:T(1,128)} %reshape.315), calls=%async_computation.1 | async-start | bytes 524288 | tf_op jit(solution)/shard_map/all_to_all | solution.py:345
  105.3 2.1 %collective-permute-start.7 = (f32[16,8,256]{2,1,0:T(8,128)S(1)}, f32[16,8,256]{2,1,0:T(8,128)S(1)}, u32[]{:S(2)}, u32[]{:S(2)}) collective-permute-start(f32[16,8,256]{2,1,0:T(8,128)S(1)} %get-tuple-element.27), channel_id=1, source_target_pairs={{0,2},{2,0},{4,6},{6,4},{8,10},{10,8},{12,14},{14,12},{1,3},{3,1},... | collective-permute-start | bytes 393224 | tf_op jit(solution)/shard_map/ppermute | solution.py:339
  107.3 0.7 maximum_select_fusion.7
  108.1 3.7 %collective-permute-done.7 = f32[16,8,256]{2,1,0:T(8,128)S(1)} collective-permute-done((f32[16,8,256]{2,1,0:T(8,128)S(1)}, f32[16,8,256]{2,1,0:T(8,128)S(1)}, u32[]{:S(2)}, u32[]{:S(2)}) %collective-permute-start.7) | collective-permute-done | bytes 131104 | tf_op jit(solution)/shard_map/ppermute | solution.py:339
  111.8 0.7 maximum_select_fusion.6
  112.5 0.9 all-to-all-done.1
  113.4 1.2 reduce.1
  114.6 0.3 reshape.316
  115.1 1.8 %fusion.8 = f32[64,2,16,32,1]{0,3,2,1,4:T(8,128)S(1)} fusion(f32[4,2,16,16,32]{4,3,2,1,0:T(8,128)S(1)} %reverse_select_fusion, f32[64]{0:T(128)S(1)} %exponential_reduce_fusion, f32[4,16]{1,0:T(4,128)S(1)} %add_convert_fusion, f32[64]{0:T(128)S(1)} %iota_convert_fusion), kind=kOutput, calls=%fused_computation.31 | convolution fusion | flops 50352128 | bytes 525056 | tf_op jit(solution)/shard_map/phixz,ypx->zhiy/dot_general | solution.py:353
  116.9 1.1 copy.65
  (45 shorter events, 0.8 us)
Async XLA Ops:
  0.7 4.1 %copy-start.1 = (f32[32,8,256]{2,1,0:T(8,128)S(1)}, f32[32,8,256]{2,1,0:T(8,128)}, u32[]{:S(2)}) copy-start(f32[32,8,256]{2,1,0:T(8,128)} %param.13) | copy-start | bytes 786436
  1.7 3.2 %copy-start.2 = (f32[32,8,256]{2,1,0:T(8,128)S(1)}, f32[32,8,256]{2,1,0:T(8,128)}, u32[]{:S(2)}) copy-start(f32[32,8,256]{2,1,0:T(8,128)} %param.14) | copy-start | bytes 786436
  1.7 23.8 %collective-permute-start.1 = (f32[16,8,256]{2,1,0:T(8,128)S(1)}, f32[16,8,256]{2,1,0:T(8,128)S(1)}, u32[]{:S(2)}, u32[]{:S(2)}) collective-permute-start(f32[16,8,256]{2,1,0:T(8,128)S(1)} %get-tuple-element.37), channel_id=1, source_target_pairs={{0,2},{2,0},{4,6},{6,4},{8,10},{10,8},{12,14},{14,12},{1,3},{3,1},... | collective-permute-start | bytes 393224 | tf_op jit(solution)/shard_map/ppermute | solution.py:276
  4.8 2.2 %copy-start.3 = (f32[32,8,256]{2,1,0:T(8,128)S(1)}, f32[32,8,256]{2,1,0:T(8,128)}, u32[]{:S(2)}) copy-start(f32[32,8,256]{2,1,0:T(8,128)} %param.15) | copy-start | bytes 786436
  4.8 21.6 %collective-permute-start.2 = (f32[16,8,256]{2,1,0:T(8,128)S(1)}, f32[16,8,256]{2,1,0:T(8,128)S(1)}, u32[]{:S(2)}, u32[]{:S(2)}) collective-permute-start(f32[16,8,256]{2,1,0:T(8,128)S(1)} %get-tuple-element.35), channel_id=1, source_target_pairs={{0,2},{2,0},{4,6},{6,4},{8,10},{10,8},{12,14},{14,12},{1,3},{3,1},... | collective-permute-start | bytes 393224 | tf_op jit(solution)/shard_map/ppermute | solution.py:276
  4.9 22.2 %collective-permute-start.3 = (f32[16,8,256]{2,1,0:T(8,128)S(1)}, f32[16,8,256]{2,1,0:T(8,128)S(1)}, u32[]{:S(2)}, u32[]{:S(2)}) collective-permute-start(f32[16,8,256]{2,1,0:T(8,128)S(1)} %get-tuple-element.33), channel_id=1, source_target_pairs={{0,2},{2,0},{4,6},{6,4},{8,10},{10,8},{12,14},{14,12},{1,3},{3,1},... | collective-permute-start | bytes 393224 | tf_op jit(solution)/shard_map/ppermute | solution.py:276
  7.0 0.7 copy-start.9
  7.0 20.8 %collective-permute-start.4 = (f32[16,8,256]{2,1,0:T(8,128)S(1)}, f32[16,8,256]{2,1,0:T(8,128)S(1)}, u32[]{:S(2)}, u32[]{:S(2)}) collective-permute-start(f32[16,8,256]{2,1,0:T(8,128)S(1)} %get-tuple-element.31), channel_id=1, source_target_pairs={{0,2},{2,0},{4,6},{6,4},{8,10},{10,8},{12,14},{14,12},{1,3},{3,1},... | collective-permute-start | bytes 393224 | tf_op jit(solution)/shard_map/ppermute | solution.py:276
  7.7 0.7 copy-start.8
  7.7 2.1 %copy-start.7 = (f32[8,128]{1,0:T(8,128)S(1)}, f32[8,128]{1,0:T(8,128)}, u32[]{:S(2)}) copy-start(f32[8,128]{1,0:T(8,128)} %param.17) | copy-start | bytes 12292
  8.4 10.7 %collective-permute-start.6 = (s32[2,128]{1,0:T(2,128)S(1)}, s32[2,128]{1,0:T(2,128)S(1)}, u32[]{:S(2)}, u32[]{:S(2)}) collective-permute-start(s32[2,128]{1,0:T(2,128)S(1)} %pad_add_fusion), channel_id=1, source_target_pairs={{0,2},{2,0},{4,6},{6,4},{8,10},{10,8},{12,14},{14,12},{1,3},{3,1},... | collective-permute-start | bytes 3080 | tf_op jit(solution)/shard_map/ppermute | solution.py:285
  10.1 5.9 %copy-start.4 = (f32[32,8,256]{2,1,0:T(8,128)S(1)}, f32[32,8,256]{2,1,0:T(8,128)}, u32[]{:S(2)}) copy-start(f32[32,8,256]{2,1,0:T(8,128)} %param.16) | copy-start | bytes 786436
  10.9 12.6 %all-to-all-start = ((f32[16,1,128]{2,1,0:T(1,128)}), f32[16,1,128]{2,1,0:T(1,128)S(1)}, u32[]{:S(2)}, u32[]{:S(2)}) async-start(f32[16,1,128]{2,1,0:T(1,128)} %reshape.313), calls=%async_computation | async-start | bytes 16384 | tf_op jit(solution)/shard_map/all_to_all | solution.py:280
  16.0 1.0 copy-start.5
  17.0 0.7 copy-start.10
  19.1 9.5 %collective-permute-start.5 = (f32[16,8,256]{2,1,0:T(8,128)S(1)}, f32[16,8,256]{2,1,0:T(8,128)S(1)}, u32[]{:S(2)}, u32[]{:S(2)}) collective-permute-start(f32[16,8,256]{2,1,0:T(8,128)S(1)} %get-tuple-element.29), channel_id=1, source_target_pairs={{0,2},{2,0},{4,6},{6,4},{8,10},{10,8},{12,14},{14,12},{1,3},{3,1},... | collective-permute-start | bytes 393224 | tf_op jit(solution)/shard_map/ppermute | solution.py:276
  25.6 5.3 %collective-permute-start = (f32[16,8,256]{2,1,0:T(8,128)S(1)}, f32[16,8,256]{2,1,0:T(8,128)S(1)}, u32[]{:S(2)}, u32[]{:S(2)}) collective-permute-start(f32[16,8,256]{2,1,0:T(8,128)S(1)} %get-tuple-element.39), channel_id=1, source_target_pairs={{0,2},{2,0},{4,6},{6,4},{8,10},{10,8},{12,14},{14,12},{1,3},{3,1},... | collective-permute-start | bytes 393224 | tf_op jit(solution)/shard_map/ppermute | solution.py:276
  97.0 3.0 %copy-start = (f32[16,16,256]{2,1,0:T(8,128)S(1)}, f32[16,16,256]{2,1,0:T(8,128)}, u32[]{:S(2)}) copy-start(f32[16,16,256]{2,1,0:T(8,128)} %get-tuple-element.6) | copy-start | bytes 786436
  98.0 9.3 %collective-permute-start.8 = (f32[16,8,256]{2,1,0:T(8,128)S(1)}, f32[16,8,256]{2,1,0:T(8,128)S(1)}, u32[]{:S(2)}, u32[]{:S(2)}) collective-permute-start(f32[16,8,256]{2,1,0:T(8,128)S(1)} %get-tuple-element.25), channel_id=1, source_target_pairs={{0,2},{2,0},{4,6},{6,4},{8,10},{10,8},{12,14},{14,12},{1,3},{3,1},... | collective-permute-start | bytes 393224 | tf_op jit(solution)/shard_map/ppermute | solution.py:339
  101.6 3.6 %copy-start.6 = (f32[16,16,256]{2,1,0:T(8,128)S(1)}, f32[16,16,256]{2,1,0:T(8,128)}, u32[]{:S(2)}) copy-start(f32[16,16,256]{2,1,0:T(8,128)} %get-tuple-element.7) | copy-start | bytes 786436
  101.6 11.8 %all-to-all-start.1 = ((f32[8,1,8192]{2,1,0:T(1,128)}), f32[8,1,8192]{2,1,0:T(1,128)S(1)}, u32[]{:S(2)}, u32[]{:S(2)}) async-start(f32[8,1,8192]{2,1,0:T(1,128)} %reshape.315), calls=%async_computation.1 | async-start | bytes 524288 | tf_op jit(solution)/shard_map/all_to_all | solution.py:345
  105.3 6.5 %collective-permute-start.7 = (f32[16,8,256]{2,1,0:T(8,128)S(1)}, f32[16,8,256]{2,1,0:T(8,128)S(1)}, u32[]{:S(2)}, u32[]{:S(2)}) collective-permute-start(f32[16,8,256]{2,1,0:T(8,128)S(1)} %get-tuple-element.27), channel_id=1, source_target_pairs={{0,2},{2,0},{4,6},{6,4},{8,10},{10,8},{12,14},{14,12},{1,3},{3,1},... | collective-permute-start | bytes 393224 | tf_op jit(solution)/shard_map/ppermute | solution.py:339
where the time goes:
time: 118 us
  Pallas kernels  65.4 us (55%)
  starting transfers between devices  21.4 us (18%)
  local copies, waits for them, and re-layouts  12.1 us (10%)
  other arithmetic  10.1 us (9%)
  waiting for transfers between devices  6.2 us (5%)
  matrix products  1.84 us (2%)
    pallas_call x1, Pallas kernels, per_device(): pl.pallas_call(kernel, out_shape=[jax.ShapeDtypeStruct(block, jnp.float32...  65.4 us
    ppermute x6, starting transfers between devices, gather_pair(): return pair_up(kept, lax.ppermute(sent, 'xline', swap), 1)  7.31 us
    unnamed x27, local copies, waits for them, and re-layouts  6.08 us
    all_to_all x1, starting transfers between devices, per_device(): lax.all_to_all(columns.reshape(steps, -1), ('xline', 'inline'), split_axi...  5 us
    select_n x7, other arithmetic, pair_up(): jnp.where(side == 0, jnp.concatenate([mine, theirs], axis=axis), jnp.conc...  4.35 us
    ppermute x2, starting transfers between devices, split_pair(): got = lax.ppermute(sent, 'xline', swap)  4.02 us
    ppermute x2, waiting for transfers between devices, split_pair(): got = lax.ppermute(sent, 'xline', swap)  3.73 us
    all_to_all x1, starting transfers between devices, per_device(): lax.all_to_all(raw.reshape(n_i, n_x, pieces, depth // pieces).transpose(2...  3.61 us
  transfers between devices with their start and end apart: 11, of which 3 were waited for; matrix products, arithmetic and copies ran while one was open for 12% of the time, Pallas kernels for 0%

commit v1 on v0

v1 whole, which is shorter than its diff:
```python
import functools

import jax
import jax.numpy as jnp
from jax import lax
from jax.experimental import pallas as pl
from jax.experimental.pallas import tpu as pltpu
from jax.sharding import PartitionSpec as P

CAP = 8
SMOOTH = 16
MESH = pl.DeviceIdType.MESH

SECOND_COEFFS = (-205.0 / 72.0, 8.0 / 5.0, -1.0 / 5.0, 8.0 / 315.0, -1.0 / 560.0)
FIRST_COEFFS = (4.0 / 5.0, -1.0 / 5.0, 4.0 / 105.0, -1.0 / 280.0)
LEFT, RIGHT, UP, DOWN = 0, 1, 2, 3
DENSITY = 4
RHO, NOW, SPEED, BEFORE, ADJ_NOW, ADJ_BEFORE = range(6)


def split_bf16(value):
    high = value.astype(jnp.bfloat16)
    low = (value - high.astype(jnp.float32)).astype(jnp.bfloat16)
    return high, low


def dot(a, b):
    return jnp.dot(a, b, preferred_element_type=jnp.float32)


def dot_nt(a, b):
    return lax.dot_general(a, b, (((1,), (1,)), ((), ())), preferred_element_type=jnp.float32)


def dot_tn_exact(a, b):
    dims = (((0,), (0,)), ((), ()))
    ah, al = split_bf16(a)
    bh, bl = split_bf16(b)
    one = lax.dot_general(ah, bh, dims, preferred_element_type=jnp.float32)
    two = lax.dot_general(al, bh, dims, preferred_element_type=jnp.float32)
    three = lax.dot_general(ah, bl, dims, preferred_element_type=jnp.float32)
    return one + (two + three)


def div(value, n):
    return lax.shift_right_arithmetic(value, jnp.full_like(value, n.bit_length() - 1))


def mod(value, n):
    return value & (n - 1)


def wave_kernel(
    sizes,
    log_density, fwd_now, velocity, fwd_before, adj_now, adj_before,
    observed, rec_cells, rec_counts, src_cell, wavelet,
    grad_out, last_out, previous_out,
    field, vel, x_in, x_out, i_in, accel, base, image, slopes, speed_sq, wx,
    row_map, zmap_t, z_mat, residual_ref, traces, list_out, list_in, obs_in, g_send, g_in, kern_t,
    send_sem, recv_sem, rt_send, rt_recv, rt_local, list_send, list_recv, obs_send, obs_recv,
    ret_send, ret_recv, ret_local, g_ssem, g_rsem,
):
    tile_i, tile_x, n_i, n_x, depth, steps, n_xline, fused = sizes
    rows = n_i * n_x
    slots = rec_cells.shape[1]
    n_group = 2 * n_xline
    xl = lax.axis_index("xline")
    core = lax.axis_index("inline")
    me = xl * 2 + core
    y = lax.rem(xl, 2)
    plane = xl // 2
    z_odd = lax.rem(plane, 2)
    mate = xl + 1 - 2 * y
    cp = lax.rem(core + z_odd, 2)
    origin = lax.rem(y + cp, 2)
    q = 2 * origin + cp
    stays = y == z_odd
    has = (xl >= 2, xl < n_xline - 2, q > 0, q < 3)
    other_core = 1 - core
    target = (
        {"xline": xl - 2, "inline": other_core},
        {"xline": xl + 2, "inline": other_core},
        {"xline": jnp.where(q == 2, xl, mate), "inline": other_core},
        {"xline": jnp.where(q == 1, xl, mate), "inline": other_core},
    )
    inner_i = pl.ds(4, n_i)
    inner_x = pl.ds(8, n_x)
    middle = n_i // 2

    barrier = pltpu.get_barrier_semaphore()

    @pl.loop(1, n_group)
    def _(r):
        peer = lax.rem(me + r, n_group)
        pl.semaphore_signal(
            barrier, inc=1, device_id={"xline": peer // 2, "inline": lax.rem(peer, 2)}, device_id_type=MESH
        )

    def copy_of(idx, way, part):
        part_rows = pl.ds(part * middle, middle)
        sem = way
        if way == LEFT:
            src, dst = x_out.at[idx, 0, part_rows], x_in.at[idx, 1, part_rows]
            sem = way + 4 * part
        elif way == RIGHT:
            src, dst = x_out.at[idx, 1, part_rows], x_in.at[idx, 0, part_rows]
            sem = way + 4 * part
        elif way == UP:
            src, dst = field.at[idx, pl.ds(4, 4), inner_x, :], i_in.at[idx, 1]
        else:
            src, dst = field.at[idx, pl.ds(n_i, 4), inner_x, :], i_in.at[idx, 0]
        return pltpu.make_async_remote_copy(
            src_ref=src, dst_ref=dst,
            send_sem=send_sem.at[idx, sem], recv_sem=recv_sem.at[idx, sem],
            device_id=target[way], device_id_type=MESH,
        )

    def send(idx, part):
        for way in (LEFT, RIGHT, UP + part):
            @pl.when(has[way])
            def _():
                copy_of(idx, way, part).start()

    def stage(idx, part):
        part_rows = pl.ds(part * middle, middle)
        field_rows = pl.ds(4 + part * middle, middle)
        x_out[idx, 0, part_rows] = field[idx, field_rows, pl.ds(8, 4), :]
        x_out[idx, 1, part_rows] = field[idx, field_rows, pl.ds(4 + n_x, 4), :]

    def finish(idx, part):
        for way in (LEFT, RIGHT, UP + part):
            @pl.when(has[way])
            def _():
                copy_of(idx, way, part).wait_send()
                copy_of(idx, way ^ 1, part).wait_recv()

    sources = (log_density, fwd_now, velocity, fwd_before, adj_now, adj_before)
    places = (DENSITY, 0, None, 1, 2, 3)

    def landing(n, from_y):
        columns = pl.multiple_of(from_y * tile_x, tile_x)
        if n == SPEED:
            return vel.at[:, pl.ds(columns, tile_x), :]
        return field.at[places[n], inner_i, pl.ds(pl.multiple_of(8 + columns, 8), tile_x), :]

    def tile_copy(n, a):
        return pltpu.make_async_remote_copy(
            src_ref=sources[n].at[pl.ds(a * n_i, n_i)], dst_ref=landing(n, y),
            send_sem=rt_send.at[n, a], recv_sem=rt_recv.at[n, y],
            device_id={"xline": 2 * plane + lax.rem(core + a, 2), "inline": lax.rem(a + z_odd, 2)},
            device_id_type=MESH,
        )

    def tile_arrival(n, from_y):
        return pltpu.make_async_remote_copy(
            src_ref=sources[n].at[pl.ds(0, n_i)], dst_ref=landing(n, from_y),
            send_sem=rt_send.at[n, 0], recv_sem=rt_recv.at[n, from_y],
            device_id={"xline": mate}, device_id_type=MESH,
        )

    def own_copy(n):
        return pltpu.make_async_copy(
            sources[n].at[pl.ds(cp * n_i, n_i)], landing(n, y), rt_local.at[n]
        )

    def leaves(a):
        return jnp.logical_not(jnp.logical_and(stays, cp == a))

    def arrives(from_y):
        return jnp.logical_not(jnp.logical_and(stays, y == from_y))

    def tile_start(n):
        for a in range(2):
            @pl.when(leaves(a))
            def _():
                tile_copy(n, a).start()

        @pl.when(stays)
        def _():
            own_copy(n).start()

    def tile_finish(n):
        for from_y in range(2):
            @pl.when(arrives(from_y))
            def _():
                tile_arrival(n, from_y).wait_recv()
        for a in range(2):
            @pl.when(leaves(a))
            def _():
                tile_copy(n, a).wait_send()

        @pl.when(stays)
        def _():
            own_copy(n).wait()

    def list_copy(a):
        return pltpu.make_async_remote_copy(
            src_ref=list_out, dst_ref=list_in.at[y],
            send_sem=list_send.at[a], recv_sem=list_recv.at[y],
            device_id={"xline": 2 * plane + lax.rem(core + a, 2), "inline": lax.rem(a + z_odd, 2)},
            device_id_type=MESH,
        )

    def list_arrival(from_y):
        return pltpu.make_async_remote_copy(
            src_ref=list_out, dst_ref=list_in.at[from_y],
            send_sem=list_send.at[0], recv_sem=list_recv.at[from_y],
            device_id={"xline": mate}, device_id_type=MESH,
        )

    def obs_copy(peer, slot):
        return pltpu.make_async_remote_copy(
            src_ref=observed, dst_ref=obs_in.at[slot],
            send_sem=obs_send.at[peer], recv_sem=obs_recv.at[slot],
            device_id={"xline": peer // 2, "inline": lax.rem(peer, 2)}, device_id_type=MESH,
        )

    finals = (previous_out, last_out)
    final_idx = (2 + (steps - 1) % 2, 2 + steps % 2)

    def home_copy(n, to_y):
        return pltpu.make_async_remote_copy(
            src_ref=field.at[final_idx[n], inner_i, pl.ds(8 + to_y * tile_x, tile_x), :],
            dst_ref=finals[n].at[pl.ds(cp * n_i, n_i)],
            send_sem=ret_send.at[n, to_y], recv_sem=ret_recv.at[n, cp],
            device_id={"xline": 2 * plane + to_y, "inline": origin}, device_id_type=MESH,
        )

    def home_arrival(n, a):
        return pltpu.make_async_remote_copy(
            src_ref=field.at[final_idx[n], inner_i, pl.ds(8, tile_x), :],
            dst_ref=finals[n].at[pl.ds(a * n_i, n_i)],
            send_sem=ret_send.at[n, 0], recv_sem=ret_recv.at[n, a],
            device_id={"xline": mate}, device_id_type=MESH,
        )

    def home_own(n):
        columns = pl.multiple_of(8 + y * tile_x, 8)
        return pltpu.make_async_copy(
            field.at[final_idx[n], inner_i, pl.ds(columns, tile_x), :],
            finals[n].at[pl.ds(cp * n_i, n_i)], ret_local.at[n],
        )

    def home_start(n):
        for to_y in range(2):
            @pl.when(arrives(to_y))
            def _():
                home_copy(n, to_y).start()

        @pl.when(stays)
        def _():
            home_own(n).start()

    def home_finish(n):
        for to_y in range(2):
            @pl.when(arrives(to_y))
            def _():
                home_copy(n, to_y).wait_send()
        for a in range(2):
            @pl.when(leaves(a))
            def _():
                home_arrival(n, a).wait_recv()

        @pl.when(stays)
        def _():
            home_own(n).wait()

    dz = depth // n_xline
    planes_n = n_xline // 2

    def slab_copy(d):
        return pltpu.make_async_remote_copy(
            src_ref=g_send.at[d],
            dst_ref=g_in.at[cp, :, pl.ds(pl.multiple_of(plane * n_x, 8), n_x), :],
            send_sem=g_ssem.at[d], recv_sem=g_rsem.at[cp, plane],
            device_id={"xline": d, "inline": origin}, device_id_type=MESH,
        )

    def slab_arrival(a, p):
        return pltpu.make_async_remote_copy(
            src_ref=g_send.at[0],
            dst_ref=g_in.at[a, :, pl.ds(pl.multiple_of(p * n_x, 8), n_x), :],
            send_sem=g_ssem.at[0], recv_sem=g_rsem.at[a, p],
            device_id={"xline": mate}, device_id_type=MESH,
        )

    def fused_gradient():
        group = 128 // dz
        lane = div(lax.broadcasted_iota(jnp.int32, (n_x, 128), 1), dz)
        for chunk in range(depth // 128):
            for ig in range(n_i // group):
                planes = [image[ig * group + j, :, pl.ds(chunk * 128, 128)] for j in range(group)]
                for dd in range(group):
                    out = None
                    for j in range(group):
                        shift = (j - dd) * dz % 128
                        moved = pltpu.roll(planes[j], shift, axis=1) if shift else planes[j]
                        out = moved if out is None else jnp.where(lane == j, moved, out)
                    g_send[chunk * group + dd, ig] = out

        @pl.loop(1, n_xline + 1)
        def _(r):
            d = lax.rem(xl + r, n_xline)

            @pl.when(jnp.logical_or(d != xl, origin != core))
            def _():
                slab_copy(d).start()

        home_start(1)

        @pl.when(origin == core)
        def _():
            g_in[cp, :, pl.ds(pl.multiple_of(plane * n_x, 8), n_x), :] = g_send[xl]

        @pl.loop(0, n_xline)
        def _(r):
            a, p = lax.rem(r, 2), r // 2
            mine = jnp.logical_and(origin == core, jnp.logical_and(a == cp, p == plane))

            @pl.when(jnp.logical_not(mine))
            def _():
                slab_arrival(a, p).wait_recv()

        for a in range(2):
            for ig in range(n_i // group):
                lines = dot_tn_exact(g_in[a, ig], kern_t[...])
                for j in range(group):
                    grad_out[a * n_i + ig * group + j] = lines[j * dz:(j + 1) * dz]

        @pl.loop(1, n_xline + 1)
        def _(r):
            d = lax.rem(xl + r, n_xline)

            @pl.when(jnp.logical_or(d != xl, origin != core))
            def _():
                slab_copy(d).wait_send()

    for idx in range(5):
        field[idx, pl.ds(0, 4)] = jnp.zeros((4,) + field.shape[2:], jnp.float32)
        field[idx, pl.ds(n_i + 4, 4)] = jnp.zeros((4,) + field.shape[2:], jnp.float32)
        field[idx, inner_i, pl.ds(0, 8)] = jnp.zeros((n_i, 8, depth), jnp.float32)
        field[idx, inner_i, pl.ds(8 + n_x, 8)] = jnp.zeros((n_i, 8, depth), jnp.float32)
    for way in (LEFT, RIGHT, UP, DOWN):
        @pl.when(jnp.logical_not(has[way]))
        def _():
            halo = x_in if way < UP else i_in
            halo[:, way % 2] = jnp.zeros(halo.shape[:1] + halo.shape[2:], jnp.float32)
    image[...] = jnp.zeros(image.shape, jnp.float32)
    accel[steps] = jnp.zeros(accel.shape[1:], jnp.float32)

    n_counts = rec_counts.shape[1]
    spread = (
        div(lax.broadcasted_iota(jnp.int32, (n_counts, slots), 1), CAP)
        == lax.broadcasted_iota(jnp.int32, (n_counts, slots), 0)
    ).astype(jnp.float32).astype(jnp.bfloat16)
    counts = jnp.broadcast_to(rec_counts[...].astype(jnp.float32), (8, n_counts)).astype(jnp.bfloat16)
    live = dot(counts, spread)
    place = mod(lax.broadcasted_iota(jnp.int32, (8, slots), 1), CAP).astype(jnp.float32)
    list_out[...] = jnp.where(place < live, jnp.broadcast_to(rec_cells[...], (8, slots)), -1)

    pl.semaphore_wait(barrier, n_group - 1)

    for n in (RHO, NOW):
        tile_start(n)
    for a in range(2):
        @pl.when(leaves(a))
        def _():
            list_copy(a).start()

    for n in (SPEED, BEFORE):
        tile_start(n)

    @pl.loop(1, n_group)
    def _(r):
        obs_copy(lax.rem(me + r, n_group), me).start()

    obs_in[me] = observed[...]

    @pl.when(stays)
    def _():
        list_in[y] = list_out[...]

    offset = lax.broadcasted_iota(jnp.int32, (depth, depth), 0) - lax.broadcasted_iota(jnp.int32, (depth, depth), 1)
    second = jnp.zeros((depth, depth), jnp.float32)
    first = jnp.zeros((depth, depth), jnp.float32)
    for k in range(1, 5):
        second = jnp.where((offset == k) | (offset == -k), SECOND_COEFFS[k] / SECOND_COEFFS[1], second)
        first = jnp.where(offset == k, FIRST_COEFFS[k - 1] / FIRST_COEFFS[0], first)
        first = jnp.where(offset == -k, -FIRST_COEFFS[k - 1] / FIRST_COEFFS[0], first)
    z_mat[:, pl.ds(0, depth)] = second.astype(jnp.bfloat16)
    z_mat[:, pl.ds(depth, depth)] = first.astype(jnp.bfloat16)

    full_x = tile_x * n_xline
    cells = src_cell[...]
    src_i = div(cells, full_x * depth) - q * n_i
    src_x = mod(div(cells, depth), full_x) - plane * n_x
    inside = (src_i >= 0) & (src_i < n_i) & (src_x >= 0) & (src_x < n_x)
    src_row = jnp.where(inside, src_i * n_x + src_x, -1)
    n_src = cells.shape[1]
    src_rows = (lax.broadcasted_iota(jnp.int32, (rows, n_src), 0) == src_row).astype(jnp.float32)
    src_cols = (lax.broadcasted_iota(jnp.int32, (depth, n_src), 0) == mod(cells, depth)).astype(jnp.float32).astype(jnp.bfloat16)

    if fused:
        far = (
            lax.broadcasted_iota(jnp.int32, (full_x, full_x), 0) - lax.broadcasted_iota(jnp.int32, (full_x, full_x), 1)
        ).astype(jnp.float32)
        weights = jnp.exp(-jnp.abs(far) / SMOOTH)
        kern_t[...] = weights / jnp.sum(weights, axis=0, keepdims=True)

    def flat(idx):
        return field[idx, inner_i, inner_x, :].reshape(rows, depth)

    def along_depth(idx):
        high, low = split_bf16(flat(idx))
        both = dot(high, z_mat[...]) + dot(low, z_mat[...])
        return both[:, :depth], both[:, depth:]

    def across(idx, i):
        lap = slope_i = slope_x = None
        for k in range(1, 5):
            plus_i = field[idx, i + 4 + k, inner_x, :]
            minus_i = field[idx, i + 4 - k, inner_x, :]
            plus_x = field[idx, i + 4, pl.ds(8 + k, n_x), :]
            minus_x = field[idx, i + 4, pl.ds(8 - k, n_x), :]
            terms = (
                SECOND_COEFFS[k] * ((plus_i + minus_i) + (plus_x + minus_x)),
                FIRST_COEFFS[k - 1] * (plus_i - minus_i),
                FIRST_COEFFS[k - 1] * (plus_x - minus_x),
            )
            if lap is None:
                lap, slope_i, slope_x = terms
            else:
                lap, slope_i, slope_x = lap + terms[0], slope_i + terms[1], slope_x + terms[2]
        return lap, slope_i, slope_x

    tile_finish(RHO)
    for part in range(2):
        stage(DENSITY, part)
        send(DENSITY, part)
    tile_finish(NOW)
    for part in range(2):
        stage(0, part)
        send(0, part)

    slopes[2] = (FIRST_COEFFS[0] * FIRST_COEFFS[0] * along_depth(DENSITY)[1]).reshape(n_i, n_x, depth)

    for from_y in range(2):
        @pl.when(arrives(from_y))
        def _():
            list_arrival(from_y).wait_recv()
    for a in range(2):
        @pl.when(leaves(a))
        def _():
            list_copy(a).wait_send()
    for from_y in range(2):
        spot = list_in[from_y][:1]
        cell_i = div(spot, tile_x * depth) - cp * n_i
        cell_x = mod(div(spot, depth), tile_x) + from_y * tile_x
        row = jnp.where((spot >= 0) & (cell_i >= 0) & (cell_i < n_i), cell_i * n_x + cell_x, -1)
        columns = pl.ds(from_y * slots, slots)
        row_map[:, columns] = (lax.broadcasted_iota(jnp.int32, (rows, slots), 0) == row).astype(jnp.float32)
        zmap_t[:, columns] = (
            lax.broadcasted_iota(jnp.int32, (depth, slots), 0) == mod(spot, depth)
        ).astype(jnp.float32).astype(jnp.bfloat16)

    finish(DENSITY, 0)
    finish(DENSITY, 1)
    field[DENSITY, pl.ds(0, 4), inner_x, :] = i_in[DENSITY, 0]
    field[DENSITY, pl.ds(n_i + 4, 4), inner_x, :] = i_in[DENSITY, 1]
    field[DENSITY, inner_i, pl.ds(4, 4), :] = x_in[DENSITY, 0]
    field[DENSITY, inner_i, pl.ds(8 + n_x, 4), :] = x_in[DENSITY, 1]

    @pl.loop(0, n_i)
    def _(i):
        _, slope_i, slope_x = across(DENSITY, i)
        slopes[0, i] = slope_i
        slopes[1, i] = slope_x

    tile_finish(SPEED)
    speed_sq[...] = vel[...] * vel[...]
    column = lax.broadcasted_iota(jnp.int32, (n_x, depth), 0)

    @pl.loop(0, n_i)
    def _(i):
        for k in range(1, 5):
            weight = jnp.where(
                column < k, SECOND_COEFFS[k] + FIRST_COEFFS[k - 1] * slopes[1, i],
                jnp.where(column >= n_x - k, SECOND_COEFFS[k] - FIRST_COEFFS[k - 1] * slopes[1, i], 0.0),
            )
            wx[k - 1, i] = speed_sq[i] * weight

    tile_finish(BEFORE)

    def prepare(idx, term):
        lap, slope = along_depth(idx)
        partial = term + speed_sq[...].reshape(rows, depth) * (
            SECOND_COEFFS[1] * lap - slopes[2].reshape(rows, depth) * slope
        )
        base[...] = partial.reshape(n_i, n_x, depth)

    def interior(now, other, i):
        lap, slope_i, slope_x = across(now, i)
        center = field[now, i + 4, inner_x, :]
        change = base[i] + speed_sq[i] * (
            3.0 * SECOND_COEFFS[0] * center + lap - slopes[0, i] * slope_i - slopes[1, i] * slope_x
        )
        field[other, i + 4, inner_x, :] = 2.0 * center - field[other, i + 4, inner_x, :] + change
        return center, change

    def correction(now, i):
        beside = jnp.concatenate([x_in[now, 1, i], x_in[now, 0, i]], axis=0)
        total = None
        for k in range(1, 5):
            pieces = [pltpu.roll(beside, k, axis=0)]
            if n_x > 16:
                pieces.append(jnp.zeros((n_x - 16, depth), jnp.float32))
            pieces.append(pltpu.roll(beside, 8 - k, axis=0))
            term = wx[k - 1, i] * jnp.concatenate(pieces, axis=0)
            total = term if total is None else total + term
        if i < 4 or i >= n_i - 4:
            lap = None
            for h in range(4):
                k = i + 4 - h if i < 4 else n_i + h - i
                if k > 4:
                    continue
                sign = 1.0 if i < 4 else -1.0
                halo = i_in[now, 0 if i < 4 else 1, h]
                terms = SECOND_COEFFS[k] * halo, (sign * FIRST_COEFFS[k - 1]) * halo
                lap, slope = terms if lap is None else (lap + terms[0], slope + terms[1])
            total = total + speed_sq[i] * (lap + slopes[0, i] * slope)
        return total

    def correct(now, other, part, t):
        for i in range(part * middle, (part + 1) * middle):
            change = correction(now, i)
            fresh = field[other, i + 4, inner_x, :] + change
            field[other, i + 4, inner_x, :] = fresh
            x_out[other, 0, i] = fresh[:4]
            x_out[other, 1, i] = fresh[n_x - 4:]
            if t is not None:
                accel[t, i] += change

    def sample(idx, t):
        high, low = split_bf16(flat(idx))
        picked = dot(high, zmap_t[...]) + dot(low, zmap_t[...])
        predicted = jnp.sum(picked * row_map[...], axis=0, keepdims=True)
        residual_ref[t] = predicted - traces[pl.ds(t, 1), :]

    @pl.loop(0, steps)
    def _(t):
        now = lax.rem(t, 2)
        other = 1 - now
        high, low = split_bf16(src_rows * wavelet[pl.ds(t, 1), :])
        prepare(now, dot_nt(high, src_cols) + dot_nt(low, src_cols))

        @pl.loop(0, n_i)
        def _(i):
            _, change = interior(now, other, i)
            accel[t, i] = change

        @pl.when(t == 1)
        def _():
            tile_start(ADJ_NOW)

            @pl.loop(1, n_group)
            def _(r):
                peer = lax.rem(me + r, n_group)
                obs_copy(peer, peer).wait_recv()
                obs_copy(peer, me).wait_send()

            lane = div(lax.broadcasted_iota(jnp.int32, (8, slots), 1), CAP)
            for from_y in range(2):
                owner = (2 * plane + from_y) * 2 + origin

                def place_one(s, total):
                    moved = pltpu.roll(obs_in[s], lax.rem(s - owner + n_group, n_group) * CAP, axis=1)
                    return jnp.where(lane == s, moved, total)

                traces[:, pl.ds(from_y * slots, slots)] = lax.fori_loop(
                    0, n_group, place_one, jnp.zeros((8, slots), jnp.float32)
                )

        @pl.when(t == 3)
        def _():
            tile_start(ADJ_BEFORE)

        @pl.when(t >= 1)
        def _():
            sample(now, t - 1)

        @pl.when(t == steps - 1)
        def _():
            tile_finish(ADJ_NOW)
            for part in range(2):
                stage(2, part)
                send(2, part)

        for part in range(2):
            finish(now, part)
            correct(now, other, part, t)

            @pl.when(t < steps - 1)
            def _():
                send(other, part)

    sample(steps % 2, steps - 1)
    tile_finish(ADJ_BEFORE)

    @pl.loop(0, steps)
    def _(j):
        now = 2 + lax.rem(j, 2)
        other = 5 - now
        t = steps - 1 - j
        high, low = split_bf16(row_map[...] * residual_ref[t])
        prepare(now, dot_nt(high, zmap_t[...]) + dot_nt(low, zmap_t[...]))

        @pl.loop(0, n_i)
        def _(i):
            center, _ = interior(now, other, i)
            image[i] += center * accel[t + 1, i]

        @pl.when(j == steps - 1)
        def _():
            home_start(0)

        for part in range(2):
            finish(now, part)
            correct(now, other, part, None)

            @pl.when(j < steps - 1)
            def _():
                send(other, part)

    @pl.loop(0, n_i)
    def _(i):
        total = image[i] + field[final_idx[1], i + 4, inner_x, :] * accel[0, i]
        image[i] = total * (2.0 / steps) / vel[i]

    if fused:
        fused_gradient()
    else:
        grad_out[...] = image[...]
        home_start(1)
    home_finish(0)
    home_finish(1)


def per_device(
    fwd_now, fwd_before, adj_now, adj_before, velocity, log_density,
    observed, rec_cells, rec_counts, src_cell, wavelet,
):
    tile_i, tile_x, depth = fwd_now.shape
    steps = wavelet.shape[0]
    n_xline = lax.axis_size("xline")
    full_x = tile_x * n_xline
    n_i, n_x = tile_i // 2, tile_x * 2
    rows = n_i * n_x
    slots = rec_cells.shape[1]
    n_group = 2 * n_xline
    dz = depth // n_xline
    fused = dz >= 8 and 128 % dz == 0 and depth % 128 == 0 and n_i % (128 // dz) == 0
    group = 128 // dz if fused else 1

    block = (n_i, n_x, depth)
    vmem = pl.BlockSpec(memory_space=pltpu.VMEM)
    anywhere = pl.BlockSpec(memory_space=pl.ANY)
    dma = pltpu.SemaphoreType.DMA
    kernel = functools.partial(wave_kernel, (tile_i, tile_x, n_i, n_x, depth, steps, n_xline, fused))
    grad_shape = (tile_i, dz, full_x) if fused else block
    if fused:
        g_shapes = (n_xline, n_i // group, n_x, 128), (2, n_i // group, full_x, 128), (full_x, full_x)
    else:
        g_shapes = ((8, 128),) * 3
    raw, last, previous = pl.pallas_call(
        kernel,
        out_shape=[
            jax.ShapeDtypeStruct(grad_shape, jnp.float32),
            jax.ShapeDtypeStruct(fwd_now.shape, jnp.float32),
            jax.ShapeDtypeStruct(fwd_now.shape, jnp.float32),
        ],
        in_specs=[anywhere] * 6 + [vmem] * 5,
        out_specs=[vmem, anywhere, anywhere],
        scratch_shapes=[
            pltpu.VMEM((5, n_i + 8, n_x + 16, depth), jnp.float32),
            pltpu.VMEM(block, jnp.float32),
            pltpu.VMEM((5, 2, n_i, 4, depth), jnp.float32),
            pltpu.VMEM((5, 2, n_i, 4, depth), jnp.float32),
            pltpu.VMEM((5, 2, 4, n_x, depth), jnp.float32),
            pltpu.VMEM((steps + 1,) + block, jnp.float32),
            pltpu.VMEM(block, jnp.float32),
            pltpu.VMEM(block, jnp.float32),
            pltpu.VMEM((3,) + block, jnp.float32),
            pltpu.VMEM(block, jnp.float32),
            pltpu.VMEM((4,) + block, jnp.float32),
            pltpu.VMEM((rows, 2 * slots), jnp.float32),
            pltpu.VMEM((depth, 2 * slots), jnp.bfloat16),
            pltpu.VMEM((depth, 2 * depth), jnp.bfloat16),
            pltpu.VMEM((steps, 1, 2 * slots), jnp.float32),
            pltpu.VMEM((steps, 2 * slots), jnp.float32),
            pltpu.VMEM((8, slots), jnp.int32),
            pltpu.VMEM((2, 8, slots), jnp.int32),
            pltpu.VMEM((n_group,) + observed.shape, jnp.float32),
            pltpu.VMEM(g_shapes[0], jnp.float32),
            pltpu.VMEM(g_shapes[1], jnp.float32),
            pltpu.VMEM(g_shapes[2], jnp.float32),
            dma((5, 6)), dma((5, 6)),
            dma((6, 2)), dma((6, 2)), dma((6,)),
            dma((2,)), dma((2,)),
            dma((n_group,)), dma((n_group,)),
            dma((2, 2)), dma((2, 2)), dma((2,)),
            dma((n_xline,)), dma((2, n_xline // 2)),
        ],
        compiler_params=pltpu.CompilerParams(
            collective_id=0, has_side_effects=True, vmem_limit_bytes=56 * 1024 * 1024
        ),
    )(
        log_density, fwd_now, velocity, fwd_before, adj_now, adj_before,
        observed, rec_cells, rec_counts, src_cell[None, :], wavelet,
    )
    if fused:
        return raw.transpose(1, 0, 2), last, previous

    places = []
    for xl in range(n_xline):
        for core in range(2):
            y, plane = xl % 2, xl // 2
            cp = (core + plane % 2) % 2
            origin = (y + cp) % 2
            places.append((xl * 2 + core, (2 * plane + cp) * 2 + origin))
    raw = lax.ppermute(raw, ("xline", "inline"), places)
    columns = lax.all_to_all(
        raw.reshape(n_i, n_x, n_xline, dz).transpose(2, 0, 1, 3),
        "xline", split_axis=0, concat_axis=0, tiled=True,
    ).reshape(n_xline // 2, 2, n_i, n_x, dz)
    positions = jnp.arange(full_x).astype(jnp.float32)
    weights = jnp.exp(-jnp.abs(positions[:, None] - positions[None, :]) / SMOOTH)
    weights = weights / jnp.sum(weights, axis=1, keepdims=True)
    gradient = jnp.einsum(
        "phixz,ypx->zhiy", columns, weights.reshape(full_x, n_xline // 2, n_x),
        precision=lax.Precision.HIGHEST,
    ).reshape(dz, tile_i, full_x)
    return gradient, last, previous


def solution(mesh):
    return jax.shard_map(
        per_device,
        mesh=mesh,
        in_specs=(
            P(("shots", "inline"), "xline", None),
            P(("shots", "inline"), "xline", None),
            P(("shots", "inline"), "xline", None),
            P(("shots", "inline"), "xline", None),
            P("inline", "xline", None),
            P("inline", "xline", None),
            P("shots", ("xline", "inline")),
            P(("xline", "inline"), None),
            P(("xline", "inline"), None),
            P("shots"),
            P("shots", None),
        ),
        out_specs=(
            P(("shots", "xline"), "inline", None),
            P(("shots", "inline"), "xline", None),
            P(("shots", "inline"), "xline", None),
        ),
        check_vma=False,
    )
```

time: 118 us -> 89.9 us (0.76)
  starting transfers between devices: 21.4 us -> 0 us
  Pallas kernels: 65.4 us -> 85.1 us
  other arithmetic: 10.1 us -> 0 us
  local copies, waits for them, and re-layouts: 12.1 us -> 3.93 us
  waiting for transfers between devices: 6.2 us -> 0 us
  matrix products: 1.84 us -> 0 us
    pallas_call x1, Pallas kernels: 65.4 us -> 85.1 us  [per_device(): pl.pallas_call(kernel, out_shape=[jax.ShapeDtypeStruct(grad_shape, jnp.fl...]
    ppermute x9 -> x0, starting transfers between devices: 12.8 us -> none  [the longest x6 7.31 us: gather_pair(): return pair_up(kept, lax.ppermute(sent, 'xline', swap), 1)]
    all_to_all x2 -> x0, starting transfers between devices: 8.61 us -> none  [the longest x1 5 us: per_device(): lax.all_to_all(columns.reshape(steps, -1), ('xline', 'inline'), split_axi...]
    select_n x11 -> x0, other arithmetic: 6.86 us -> none  [the longest x7 4.35 us: pair_up(): jnp.where(side == 0, jnp.concatenate([mine, theirs], axis=axis), jnp.conc...]
    ppermute x9 -> x0, waiting for transfers between devices: 5.27 us -> none  [the longest x2 3.73 us: split_pair(): got = lax.ppermute(sent, 'xline', swap)]
    dynamic_slice x8 -> x0, local copies, waits for them, and re-layouts: 2.19 us -> none  [the longest x6 1.13 us: gather_pair(): kept = lax.dynamic_slice_in_dim(value, half * n_i, n_i, axis=0)]
    unnamed x27 -> x7, local copies, waits for them, and re-layouts: 6.08 us -> 3.93 us
    dot_general x1 -> x0, matrix products: 1.84 us -> none  [per_device(): jnp.einsum('phixz,ypx->zhiy', columns, weights.reshape(full_x, n_xline //...]
  transfers between devices with their start and end apart: 11 -> 0, of which waited for: 3 -> 0; matrix products, arithmetic and copies ran while one was open for 12% -> 0% of each run, Pallas kernels for 0% -> 0%
where the time goes in v1:
time: 89.9 us; the launch traced here: 89.7 us
  Pallas kernels  85.1 us (95%)
  local copies, waits for them, and re-layouts  3.93 us (4%)
    pallas_call x1, Pallas kernels, per_device(): pl.pallas_call(kernel, out_shape=[jax.ShapeDtypeStruct(grad_shape, jnp.fl...  85.1 us
    unnamed x7, local copies, waits for them, and re-layouts  3.93 us

profile of v1, /device:TPU:0, one launch (start us, length us, event | category | flops | bytes accessed | tf_op | source)
XLA Modules:
  0.0 89.7 jit_solution(3142296007830129633)
XLA Ops:
  0.6 85.1 %shard_map.130 = (f32[32,32,64]{2,1,0:T(8,128)}, f32[32,8,256]{2,1,0:T(8,128)}, f32[32,8,256]{2,1,0:T(8,128)}) custom-call(f32[32,8,256]{2,1,0:T(8,128)} %log_density.1, f32[32,8,256]{2,1,0:T(8,128)} %fwd_now.1, f32[32,8,256]{2,1,0:T(8,128)} %velocity.1, f32[32,8,256]{2,1,0:T(8,128)} %fwd_before.1, f32[32,8,256]{2,1,0:T(8,128)} %adj_now.1, ...), custom_call_target="tpu_custom_call" | custom-call | tf_op jit(solution)/shard_map/pallas_call | solution.py:674
  85.7 0.0 copy-start.1
  85.7 2.2 %copy.14 = f32[32,32,64]{2,1,0:T(8,128)} copy(f32[32,32,64]{2,0,1:T(8,128)} %bitcast.2) | data formatting | bytes 524288
  87.9 0.0 copy-done.1
  87.9 0.0 copy-start
  87.9 0.7 copy.17
  88.6 0.3 copy-done
  89.0 0.7 copy.18
Async XLA Ops:
  85.7 2.2 %copy-start.1 = (f32[32,8,256]{2,1,0:T(8,128)S(1)}, f32[32,8,256]{2,1,0:T(8,128)}, u32[]{:S(2)}) copy-start(f32[32,8,256]{2,1,0:T(8,128)} %get-tuple-element.16) | copy-start | bytes 786436
  87.9 1.0 %copy-start = (f32[32,8,256]{2,1,0:T(8,128)S(1)}, f32[32,8,256]{2,1,0:T(8,128)}, u32[]{:S(2)}) copy-start(f32[32,8,256]{2,1,0:T(8,128)} %get-tuple-element.17) | copy-start | bytes 786436

commit v2 on v1

--- a/solution.py
+++ b/solution.py
@@ -72,16 +72,16 @@
     z_odd = lax.rem(plane, 2)
     mate = xl + 1 - 2 * y
     cp = lax.rem(core + z_odd, 2)
-    origin = lax.rem(y + cp, 2)
-    q = 2 * origin + cp
-    stays = y == z_odd
+    origin = y
+    q = 2 * y + cp
+    stays = y == core
     has = (xl >= 2, xl < n_xline - 2, q > 0, q < 3)
     other_core = 1 - core
     target = (
         {"xline": xl - 2, "inline": other_core},
         {"xline": xl + 2, "inline": other_core},
-        {"xline": jnp.where(q == 2, xl, mate), "inline": other_core},
-        {"xline": jnp.where(q == 1, xl, mate), "inline": other_core},
+        {"xline": jnp.where(q == 2, mate, xl), "inline": other_core},
+        {"xline": jnp.where(q == 1, mate, xl), "inline": other_core},
     )
     inner_i = pl.ds(4, n_i)
     inner_x = pl.ds(8, n_x)
@@ -96,30 +96,39 @@
             barrier, inc=1, device_id={"xline": peer // 2, "inline": lax.rem(peer, 2)}, device_id_type=MESH
         )
 
-    def copy_of(idx, way, part):
+    def beside(idx, way, part):
         part_rows = pl.ds(part * middle, middle)
-        sem = way
-        if way == LEFT:
-            src, dst = x_out.at[idx, 0, part_rows], x_in.at[idx, 1, part_rows]
-            sem = way + 4 * part
-        elif way == RIGHT:
-            src, dst = x_out.at[idx, 1, part_rows], x_in.at[idx, 0, part_rows]
-            sem = way + 4 * part
-        elif way == UP:
-            src, dst = field.at[idx, pl.ds(4, 4), inner_x, :], i_in.at[idx, 1]
-        else:
-            src, dst = field.at[idx, pl.ds(n_i, 4), inner_x, :], i_in.at[idx, 0]
-        return pltpu.make_async_remote_copy(
-            src_ref=src, dst_ref=dst,
+        sem = way + 4 * part
+        return pltpu.make_async_remote_copy(
+            src_ref=x_out.at[idx, way, part_rows], dst_ref=x_in.at[idx, 1 - way, part_rows],
             send_sem=send_sem.at[idx, sem], recv_sem=recv_sem.at[idx, sem],
             device_id=target[way], device_id_type=MESH,
         )
 
+    def above(idx, part, side):
+        up = part == 0
+        return pltpu.make_async_remote_copy(
+            src_ref=field.at[idx, pl.ds(4 + part * (n_i - 4), 4), inner_x, :],
+            dst_ref=i_in.at[idx, part if side else 1 - part],
+            send_sem=send_sem.at[idx, 2 + part], recv_sem=recv_sem.at[idx, 3 - part if side else 2 + part],
+            device_id={
+                "xline": jnp.where(up, target[UP]["xline"], target[DOWN]["xline"]), "inline": other_core
+            },
+            device_id_type=MESH,
+        )
+
+    def has_row(part):
+        return jnp.where(part == 0, q, 3 - q) > 0
+
     def send(idx, part):
-        for way in (LEFT, RIGHT, UP + part):
+        for way in (LEFT, RIGHT):
             @pl.when(has[way])
             def _():
-                copy_of(idx, way, part).start()
+                beside(idx, way, part).start()
+
+        @pl.when(has_row(part))
+        def _():
+            above(idx, part, False).start()
 
     def stage(idx, part):
         part_rows = pl.ds(part * middle, middle)
@@ -128,11 +137,18 @@
         x_out[idx, 1, part_rows] = field[idx, field_rows, pl.ds(4 + n_x, 4), :]
 
     def finish(idx, part):
-        for way in (LEFT, RIGHT, UP + part):
+        for way in (LEFT, RIGHT):
             @pl.when(has[way])
             def _():
-                copy_of(idx, way, part).wait_send()
-                copy_of(idx, way ^ 1, part).wait_recv()
+                beside(idx, way, part).wait_send()
+                beside(idx, 1 - way, part).wait_recv()
+
+        @pl.when(has_row(part))
+        def _():
+            above(idx, part, False).wait_send()
+            above(idx, part, True).wait_recv()
+
+    halves = (1 - y, y)
 
     sources = (log_density, fwd_now, velocity, fwd_before, adj_now, adj_before)
     places = (DENSITY, 0, None, 1, 2, 3)
@@ -147,7 +163,7 @@
         return pltpu.make_async_remote_copy(
             src_ref=sources[n].at[pl.ds(a * n_i, n_i)], dst_ref=landing(n, y),
             send_sem=rt_send.at[n, a], recv_sem=rt_recv.at[n, y],
-            device_id={"xline": 2 * plane + lax.rem(core + a, 2), "inline": lax.rem(a + z_odd, 2)},
+            device_id={"xline": 2 * plane + core, "inline": lax.rem(a + z_odd, 2)},
             device_id_type=MESH,
         )
 
@@ -197,7 +213,7 @@
         return pltpu.make_async_remote_copy(
             src_ref=list_out, dst_ref=list_in.at[y],
             send_sem=list_send.at[a], recv_sem=list_recv.at[y],
-            device_id={"xline": 2 * plane + lax.rem(core + a, 2), "inline": lax.rem(a + z_odd, 2)},
+            device_id={"xline": 2 * plane + core, "inline": lax.rem(a + z_odd, 2)},
             device_id_type=MESH,
         )
 
@@ -325,7 +341,7 @@
             for ig in range(n_i // group):
                 lines = dot_tn_exact(g_in[a, ig], kern_t[...])
                 for j in range(group):
-                    grad_out[a * n_i + ig * group + j] = lines[j * dz:(j + 1) * dz]
+                    grad_out[:, a * n_i + ig * group + j, :] = lines[j * dz:(j + 1) * dz]
 
         @pl.loop(1, n_xline + 1)
         def _(r):
@@ -360,13 +376,13 @@
 
     pl.semaphore_wait(barrier, n_group - 1)
 
+    for a in range(2):
+        @pl.when(leaves(a))
+        def _():
+            list_copy(a).start()
+
     for n in (RHO, NOW):
         tile_start(n)
-    for a in range(2):
-        @pl.when(leaves(a))
-        def _():
-            list_copy(a).start()
-
     for n in (SPEED, BEFORE):
         tile_start(n)
 
@@ -434,34 +450,15 @@
         return lap, slope_i, slope_x
 
     tile_finish(RHO)
-    for part in range(2):
+    for part in halves:
         stage(DENSITY, part)
         send(DENSITY, part)
     tile_finish(NOW)
-    for part in range(2):
+    for part in halves:
         stage(0, part)
         send(0, part)
 
     slopes[2] = (FIRST_COEFFS[0] * FIRST_COEFFS[0] * along_depth(DENSITY)[1]).reshape(n_i, n_x, depth)
-
-    for from_y in range(2):
-        @pl.when(arrives(from_y))
-        def _():
-            list_arrival(from_y).wait_recv()
-    for a in range(2):
-        @pl.when(leaves(a))
-        def _():
-            list_copy(a).wait_send()
-    for from_y in range(2):
-        spot = list_in[from_y][:1]
-        cell_i = div(spot, tile_x * depth) - cp * n_i
-        cell_x = mod(div(spot, depth), tile_x) + from_y * tile_x
-        row = jnp.where((spot >= 0) & (cell_i >= 0) & (cell_i < n_i), cell_i * n_x + cell_x, -1)
-        columns = pl.ds(from_y * slots, slots)
-        row_map[:, columns] = (lax.broadcasted_iota(jnp.int32, (rows, slots), 0) == row).astype(jnp.float32)
-        zmap_t[:, columns] = (
-            lax.broadcasted_iota(jnp.int32, (depth, slots), 0) == mod(spot, depth)
-        ).astype(jnp.float32).astype(jnp.bfloat16)
 
     finish(DENSITY, 0)
     finish(DENSITY, 1)
@@ -491,6 +488,45 @@
 
     tile_finish(BEFORE)
 
+    def make_maps():
+        for from_y in range(2):
+            @pl.when(arrives(from_y))
+            def _():
+                list_arrival(from_y).wait_recv()
+        for a in range(2):
+            @pl.when(leaves(a))
+            def _():
+                list_copy(a).wait_send()
+        for from_y in range(2):
+            spot = list_in[from_y][:1]
+            cell_i = div(spot, tile_x * depth) - cp * n_i
+            cell_x = mod(div(spot, depth), tile_x) + from_y * tile_x
+            row = jnp.where((spot >= 0) & (cell_i >= 0) & (cell_i < n_i), cell_i * n_x + cell_x, -1)
+            columns = pl.ds(from_y * slots, slots)
+            row_map[:, columns] = (lax.broadcasted_iota(jnp.int32, (rows, slots), 0) == row).astype(jnp.float32)
+            zmap_t[:, columns] = (
+                lax.broadcasted_iota(jnp.int32, (depth, slots), 0) == mod(spot, depth)
+            ).astype(jnp.float32).astype(jnp.bfloat16)
+
+    def make_traces():
+        @pl.loop(1, n_group)
+        def _(r):
+            peer = lax.rem(me + r, n_group)
+            obs_copy(peer, peer).wait_recv()
+            obs_copy(peer, me).wait_send()
+
+        lane = div(lax.broadcasted_iota(jnp.int32, (8, slots), 1), CAP)
+        for from_y in range(2):
+            owner = (2 * plane + from_y) * 2 + origin
+
+            def place_one(s, total):
+                moved = pltpu.roll(obs_in[s], lax.rem(s - owner + n_group, n_group) * CAP, axis=1)
+                return jnp.where(lane == s, moved, total)
+
+            traces[:, pl.ds(from_y * slots, slots)] = lax.fori_loop(
+                0, n_group, place_one, jnp.zeros((8, slots), jnp.float32)
+            )
+
     def prepare(idx, term):
         lap, slope = along_depth(idx)
         partial = term + speed_sq[...].reshape(rows, depth) * (
@@ -508,31 +544,31 @@
         return center, change
 
     def correction(now, i):
-        beside = jnp.concatenate([x_in[now, 1, i], x_in[now, 0, i]], axis=0)
+        pair = jnp.concatenate([x_in[now, 1, i], x_in[now, 0, i]], axis=0)
         total = None
         for k in range(1, 5):
-            pieces = [pltpu.roll(beside, k, axis=0)]
+            pieces = [pltpu.roll(pair, k, axis=0)]
             if n_x > 16:
                 pieces.append(jnp.zeros((n_x - 16, depth), jnp.float32))
-            pieces.append(pltpu.roll(beside, 8 - k, axis=0))
+            pieces.append(pltpu.roll(pair, 8 - k, axis=0))
             term = wx[k - 1, i] * jnp.concatenate(pieces, axis=0)
             total = term if total is None else total + term
-        if i < 4 or i >= n_i - 4:
+        return total
+
+    def correct(now, other, part, t):
+        up = part == 0
+        sign = jnp.where(up, 1.0, -1.0)
+        for r in range(middle):
+            i = jnp.where(up, r, n_i - 1 - r)
+            change = correction(now, i)
             lap = None
-            for h in range(4):
-                k = i + 4 - h if i < 4 else n_i + h - i
-                if k > 4:
-                    continue
-                sign = 1.0 if i < 4 else -1.0
-                halo = i_in[now, 0 if i < 4 else 1, h]
-                terms = SECOND_COEFFS[k] * halo, (sign * FIRST_COEFFS[k - 1]) * halo
+            for h in range(4 - r):
+                k = r + 1 + h
+                halo = i_in[now, part, jnp.where(up, 3 - h, h)]
+                terms = SECOND_COEFFS[k] * halo, FIRST_COEFFS[k - 1] * halo
                 lap, slope = terms if lap is None else (lap + terms[0], slope + terms[1])
-            total = total + speed_sq[i] * (lap + slopes[0, i] * slope)
-        return total
-
-    def correct(now, other, part, t):
-        for i in range(part * middle, (part + 1) * middle):
-            change = correction(now, i)
+            if lap is not None:
+                change = change + speed_sq[i] * (lap + (sign * slopes[0, i]) * slope)
             fresh = field[other, i + 4, inner_x, :] + change
             field[other, i + 4, inner_x, :] = fresh
             x_out[other, 0, i] = fresh[:4]
@@ -544,7 +580,7 @@
         high, low = split_bf16(flat(idx))
         picked = dot(high, zmap_t[...]) + dot(low, zmap_t[...])
         predicted = jnp.sum(picked * row_map[...], axis=0, keepdims=True)
-        residual_ref[t] = predicted - traces[pl.ds(t, 1), :]
+        residual_ref[t] = predicted
 
     @pl.loop(0, steps)
     def _(t):
@@ -561,24 +597,11 @@
         @pl.when(t == 1)
         def _():
             tile_start(ADJ_NOW)
-
-            @pl.loop(1, n_group)
-            def _(r):
-                peer = lax.rem(me + r, n_group)
-                obs_copy(peer, peer).wait_recv()
-                obs_copy(peer, me).wait_send()
-
-            lane = div(lax.broadcasted_iota(jnp.int32, (8, slots), 1), CAP)
-            for from_y in range(2):
-                owner = (2 * plane + from_y) * 2 + origin
-
-                def place_one(s, total):
-                    moved = pltpu.roll(obs_in[s], lax.rem(s - owner + n_group, n_group) * CAP, axis=1)
-                    return jnp.where(lane == s, moved, total)
-
-                traces[:, pl.ds(from_y * slots, slots)] = lax.fori_loop(
-                    0, n_group, place_one, jnp.zeros((8, slots), jnp.float32)
-                )
+            make_maps()
+
+        @pl.when(t == 4)
+        def _():
+            make_traces()
 
         @pl.when(t == 3)
         def _():
@@ -591,11 +614,11 @@
         @pl.when(t == steps - 1)
         def _():
             tile_finish(ADJ_NOW)
-            for part in range(2):
+            for part in halves:
                 stage(2, part)
                 send(2, part)
 
-        for part in range(2):
+        for part in halves:
             finish(now, part)
             correct(now, other, part, t)
 
@@ -611,7 +634,7 @@
         now = 2 + lax.rem(j, 2)
         other = 5 - now
         t = steps - 1 - j
-        high, low = split_bf16(row_map[...] * residual_ref[t])
+        high, low = split_bf16(row_map[...] * (residual_ref[t] - traces[pl.ds(t, 1), :]))
         prepare(now, dot_nt(high, zmap_t[...]) + dot_nt(low, zmap_t[...]))
 
         @pl.loop(0, n_i)
@@ -623,7 +646,7 @@
         def _():
             home_start(0)
 
-        for part in range(2):
+        for part in halves:
             finish(now, part)
             correct(now, other, part, None)
 
@@ -643,6 +666,27 @@
         home_start(1)
     home_finish(0)
     home_finish(1)
+
+
+def hand_over(*arrays):
+    count = len(arrays)
+
+    def kernel(*refs):
+        copies = [
+            pltpu.make_async_copy(refs[n], refs[count + n], refs[2 * count].at[n]) for n in range(count)
+        ]
+        for copy in copies:
+            copy.start()
+        for copy in copies:
+            copy.wait()
+
+    return pl.pallas_call(
+        kernel,
+        out_shape=[jax.ShapeDtypeStruct(array.shape, array.dtype) for array in arrays],
+        in_specs=[pl.BlockSpec(memory_space=pltpu.VMEM)] * count,
+        out_specs=[pl.BlockSpec(memory_space=pl.ANY)] * count,
+        scratch_shapes=[pltpu.SemaphoreType.DMA((count,))],
+    )(*arrays)
 
 
 def per_device(
@@ -666,7 +710,7 @@
     anywhere = pl.BlockSpec(memory_space=pl.ANY)
     dma = pltpu.SemaphoreType.DMA
     kernel = functools.partial(wave_kernel, (tile_i, tile_x, n_i, n_x, depth, steps, n_xline, fused))
-    grad_shape = (tile_i, dz, full_x) if fused else block
+    grad_shape = (dz, tile_i, full_x) if fused else block
     if fused:
         g_shapes = (n_xline, n_i // group, n_x, 128), (2, n_i // group, full_x, 128), (full_x, full_x)
     else:
@@ -718,15 +762,14 @@
         observed, rec_cells, rec_counts, src_cell[None, :], wavelet,
     )
     if fused:
-        return raw.transpose(1, 0, 2), last, previous
+        return hand_over(raw, last, previous)
 
     places = []
     for xl in range(n_xline):
         for core in range(2):
             y, plane = xl % 2, xl // 2
             cp = (core + plane % 2) % 2
-            origin = (y + cp) % 2
-            places.append((xl * 2 + core, (2 * plane + cp) * 2 + origin))
+            places.append((xl * 2 + core, (2 * plane + cp) * 2 + y))
     raw = lax.ppermute(raw, ("xline", "inline"), places)
     columns = lax.all_to_all(
         raw.reshape(n_i, n_x, n_xline, dz).transpose(2, 0, 1, 3),
@@ -739,7 +782,7 @@
         "phixz,ypx->zhiy", columns, weights.reshape(full_x, n_xline // 2, n_x),
         precision=lax.Precision.HIGHEST,
     ).reshape(dz, tile_i, full_x)
-    return gradient, last, previous
+    return (gradient,) + tuple(hand_over(last, previous))
 
 
 def solution(mesh):

time: 89.9 us -> 83.8 us (0.932); the launches traced: 89.7 us -> 82.5 us
  local copies, waits for them, and re-layouts: 3.93 us -> 0 us
  Pallas kernels: 85.1 us -> 81.9 us
    pallas_call x1, Pallas kernels: 85.1 us -> 79.7 us  [per_device(): pl.pallas_call(kernel, out_shape=[jax.ShapeDtypeStruct(grad_shape, jnp.fl...]
    unnamed x7 -> x0, local copies, waits for them, and re-layouts: 3.93 us -> none
    pallas_call x0 -> x1, Pallas kernels: none -> 2.17 us  [hand_over(): pl.pallas_call(kernel, out_shape=[jax.ShapeDtypeStruct(array.shape, array...]
where the time goes in v2:
time: 83.8 us; the launch traced here: 82.5 us
  Pallas kernels  81.9 us (98%)
    pallas_call x1, Pallas kernels, per_device(): pl.pallas_call(kernel, out_shape=[jax.ShapeDtypeStruct(grad_shape, jnp.fl...  79.7 us
    pallas_call x1, Pallas kernels, hand_over(): pl.pallas_call(kernel, out_shape=[jax.ShapeDtypeStruct(array.shape, array...  2.17 us

profile of v2, /device:TPU:0, one launch (start us, length us, event | category | flops | bytes accessed | tf_op | source)
XLA Modules:
  0.0 82.5 jit_solution(10943442229562413397)
XLA Ops:
  0.6 79.7 %shard_map.130 = (f32[32,32,64]{2,1,0:T(8,128)}, f32[32,8,256]{2,1,0:T(8,128)}, f32[32,8,256]{2,1,0:T(8,128)}) custom-call(f32[32,8,256]{2,1,0:T(8,128)} %log_density.1, f32[32,8,256]{2,1,0:T(8,128)} %fwd_now.1, f32[32,8,256]{2,1,0:T(8,128)} %velocity.1, f32[32,8,256]{2,1,0:T(8,128)} %fwd_before.1, f32[32,8,256]{2,1,0:T(8,128)} %adj_now.1, ...), custom_call_target="tpu_custom_call" | custom-call | tf_op jit(solution)/shard_map/pallas_call | solution.py:718
  80.4 2.2 %shard_map.131 = (f32[32,32,64]{2,1,0:T(8,128)}, f32[32,8,256]{2,1,0:T(8,128)}, f32[32,8,256]{2,1,0:T(8,128)}) custom-call(f32[32,32,64]{2,1,0:T(8,128)} %get-tuple-element.6.refs_0_, f32[32,8,256]{2,1,0:T(8,128)} %get-tuple-element.7.refs_1_, f32[32,8,256]{2,1,0:T(8,128)} %get-tuple-element.8.refs_2_), custom_call_target="tpu_custom_call" | custom-call | tf_op jit(solution)/shard_map/pallas_call | solution.py:683

commit v3 on v2

--- a/solution.py
+++ b/solution.py
@@ -53,16 +53,19 @@
 def wave_kernel(
     sizes,
     log_density, fwd_now, velocity, fwd_before, adj_now, adj_before,
-    observed, rec_cells, rec_counts, src_cell, wavelet,
+    given_observed, given_cells, given_counts, given_src, given_wavelet,
     grad_out, last_out, previous_out,
     field, vel, x_in, x_out, i_in, accel, base, image, slopes, speed_sq, wx,
-    row_map, zmap_t, z_mat, residual_ref, traces, list_out, list_in, obs_in, g_send, g_in, kern_t,
+    row_map, zmap_t, z_mat, residual_ref, traces, list_out, list_in, obs_in, g_send,
+    held_observed, held_cells, held_counts, held_src, held_wavelet, adj_base,
     send_sem, recv_sem, rt_send, rt_recv, rt_local, list_send, list_recv, obs_send, obs_recv,
-    ret_send, ret_recv, ret_local, g_ssem, g_rsem,
+    ret_send, ret_recv, ret_local, g_ssem, g_rsem, g_local, small_sem,
 ):
     tile_i, tile_x, n_i, n_x, depth, steps, n_xline, fused = sizes
     rows = n_i * n_x
-    slots = rec_cells.shape[1]
+    small_in = (given_observed, given_cells, given_counts, given_src, given_wavelet)
+    small_held = (held_observed, held_cells, held_counts, held_src, held_wavelet)
+    slots = held_cells.shape[1]
     n_group = 2 * n_xline
     xl = lax.axis_index("xline")
     core = lax.axis_index("inline")
@@ -89,12 +92,33 @@
 
     barrier = pltpu.get_barrier_semaphore()
 
-    @pl.loop(1, n_group)
-    def _(r):
-        peer = lax.rem(me + r, n_group)
-        pl.semaphore_signal(
-            barrier, inc=1, device_id={"xline": peer // 2, "inline": lax.rem(peer, 2)}, device_id_type=MESH
-        )
+    def greet(device):
+        pl.semaphore_signal(barrier, inc=1, device_id=device, device_id_type=MESH)
+
+    near = n_xline // 2 <= 4
+    if near:
+        greet({"inline": other_core})
+        greet({"xline": mate})
+        greet({"xline": mate, "inline": other_core})
+        for way in (LEFT, RIGHT):
+            @pl.when(has[way])
+            def _():
+                greet(target[way])
+        greeted = 3 + has[LEFT].astype(jnp.int32) + has[RIGHT].astype(jnp.int32)
+    else:
+        @pl.loop(1, n_group)
+        def _(r):
+            peer = lax.rem(me + r, n_group)
+            greet({"xline": peer // 2, "inline": lax.rem(peer, 2)})
+        greeted = n_group - 1
+
+    small = [
+        pltpu.make_async_copy(given, held, small_sem.at[n])
+        for n, (given, held) in enumerate(zip(small_in, small_held))
+    ]
+    for copy in small:
+        copy.start()
+    observed, rec_cells, rec_counts, src_cell, wavelet = small_held
 
     def beside(idx, way, part):
         part_rows = pl.ds(part * middle, middle)
@@ -287,15 +311,20 @@
     def slab_copy(d):
         return pltpu.make_async_remote_copy(
             src_ref=g_send.at[d],
-            dst_ref=g_in.at[cp, :, pl.ds(pl.multiple_of(plane * n_x, 8), n_x), :],
+            dst_ref=grad_out.at[cp, :, pl.ds(pl.multiple_of(plane * n_x, 8), n_x), :],
             send_sem=g_ssem.at[d], recv_sem=g_rsem.at[cp, plane],
             device_id={"xline": d, "inline": origin}, device_id_type=MESH,
         )
 
+    def own_slab():
+        return pltpu.make_async_copy(
+            g_send.at[xl], grad_out.at[cp, :, pl.ds(pl.multiple_of(plane * n_x, 8), n_x), :], g_local.at[0]
+        )
+
     def slab_arrival(a, p):
         return pltpu.make_async_remote_copy(
             src_ref=g_send.at[0],
-            dst_ref=g_in.at[a, :, pl.ds(pl.multiple_of(p * n_x, 8), n_x), :],
+            dst_ref=grad_out.at[a, :, pl.ds(pl.multiple_of(p * n_x, 8), n_x), :],
             send_sem=g_ssem.at[0], recv_sem=g_rsem.at[a, p],
             device_id={"xline": mate}, device_id_type=MESH,
         )
@@ -326,7 +355,7 @@
 
         @pl.when(origin == core)
         def _():
-            g_in[cp, :, pl.ds(pl.multiple_of(plane * n_x, 8), n_x), :] = g_send[xl]
+            own_slab().start()
 
         @pl.loop(0, n_xline)
         def _(r):
@@ -337,11 +366,9 @@
             def _():
                 slab_arrival(a, p).wait_recv()
 
-        for a in range(2):
-            for ig in range(n_i // group):
-                lines = dot_tn_exact(g_in[a, ig], kern_t[...])
-                for j in range(group):
-                    grad_out[:, a * n_i + ig * group + j, :] = lines[j * dz:(j + 1) * dz]
+        @pl.when(origin == core)
+        def _():
+            own_slab().wait()
 
         @pl.loop(1, n_xline + 1)
         def _(r):
@@ -362,8 +389,9 @@
             halo = x_in if way < UP else i_in
             halo[:, way % 2] = jnp.zeros(halo.shape[:1] + halo.shape[2:], jnp.float32)
     image[...] = jnp.zeros(image.shape, jnp.float32)
-    accel[steps] = jnp.zeros(accel.shape[1:], jnp.float32)
-
+
+    for copy in small:
+        copy.wait()
     n_counts = rec_counts.shape[1]
     spread = (
         div(lax.broadcasted_iota(jnp.int32, (n_counts, slots), 1), CAP)
@@ -374,7 +402,7 @@
     place = mod(lax.broadcasted_iota(jnp.int32, (8, slots), 1), CAP).astype(jnp.float32)
     list_out[...] = jnp.where(place < live, jnp.broadcast_to(rec_cells[...], (8, slots)), -1)
 
-    pl.semaphore_wait(barrier, n_group - 1)
+    pl.semaphore_wait(barrier, greeted)
 
     for a in range(2):
         @pl.when(leaves(a))
@@ -385,10 +413,6 @@
         tile_start(n)
     for n in (SPEED, BEFORE):
         tile_start(n)
-
-    @pl.loop(1, n_group)
-    def _(r):
-        obs_copy(lax.rem(me + r, n_group), me).start()
 
     obs_in[me] = observed[...]
 
@@ -415,13 +439,6 @@
     n_src = cells.shape[1]
     src_rows = (lax.broadcasted_iota(jnp.int32, (rows, n_src), 0) == src_row).astype(jnp.float32)
     src_cols = (lax.broadcasted_iota(jnp.int32, (depth, n_src), 0) == mod(cells, depth)).astype(jnp.float32).astype(jnp.bfloat16)
-
-    if fused:
-        far = (
-            lax.broadcasted_iota(jnp.int32, (full_x, full_x), 0) - lax.broadcasted_iota(jnp.int32, (full_x, full_x), 1)
-        ).astype(jnp.float32)
-        weights = jnp.exp(-jnp.abs(far) / SMOOTH)
-        kern_t[...] = weights / jnp.sum(weights, axis=0, keepdims=True)
 
     def flat(idx):
         return field[idx, inner_i, inner_x, :].reshape(rows, depth)
@@ -460,6 +477,17 @@
 
     slopes[2] = (FIRST_COEFFS[0] * FIRST_COEFFS[0] * along_depth(DENSITY)[1]).reshape(n_i, n_x, depth)
 
+    def bare(idx):
+        lap, slope = along_depth(idx)
+        return (SECOND_COEFFS[1] * lap - slopes[2].reshape(rows, depth) * slope).reshape(n_i, n_x, depth)
+
+    def inject_sources(t):
+        high, low = split_bf16(src_rows * wavelet[pl.ds(t, 1), :])
+        return dot_nt(high, src_cols) + dot_nt(low, src_cols)
+
+    base[...] = bare(0)
+    accel[0] = inject_sources(0).reshape(n_i, n_x, depth)
+
     finish(DENSITY, 0)
     finish(DENSITY, 1)
     field[DENSITY, pl.ds(0, 4), inner_x, :] = i_in[DENSITY, 0]
@@ -467,26 +495,45 @@
     field[DENSITY, inner_i, pl.ds(4, 4), :] = x_in[DENSITY, 0]
     field[DENSITY, inner_i, pl.ds(8 + n_x, 4), :] = x_in[DENSITY, 1]
 
+    def lateral(idx, i):
+        lap, slope_i, slope_x = across(idx, i)
+        center = field[idx, i + 4, inner_x, :]
+        return center, (
+            3.0 * SECOND_COEFFS[0] * center + lap - slopes[0, i] * slope_i - slopes[1, i] * slope_x
+        )
+
     @pl.loop(0, n_i)
     def _(i):
         _, slope_i, slope_x = across(DENSITY, i)
         slopes[0, i] = slope_i
         slopes[1, i] = slope_x
 
-    tile_finish(SPEED)
-    speed_sq[...] = vel[...] * vel[...]
-    column = lax.broadcasted_iota(jnp.int32, (n_x, depth), 0)
-
     @pl.loop(0, n_i)
     def _(i):
+        base[i] += lateral(0, i)[1]
+
+    tile_finish(SPEED)
+    column = lax.broadcasted_iota(jnp.int32, (n_x, depth), 0)
+
+    @pl.loop(0, n_i)
+    def _(i):
+        square = vel[i] * vel[i]
+        speed_sq[i] = square
+        accel[0, i] += square * base[i]
         for k in range(1, 5):
             weight = jnp.where(
                 column < k, SECOND_COEFFS[k] + FIRST_COEFFS[k - 1] * slopes[1, i],
                 jnp.where(column >= n_x - k, SECOND_COEFFS[k] - FIRST_COEFFS[k - 1] * slopes[1, i], 0.0),
             )
-            wx[k - 1, i] = speed_sq[i] * weight
+            wx[k - 1, i] = square * weight
 
     tile_finish(BEFORE)
+
+    @pl.loop(0, n_i)
+    def _(i):
+        field[1, i + 4, inner_x, :] = (
+            2.0 * field[0, i + 4, inner_x, :] - field[1, i + 4, inner_x, :] + accel[0, i]
+        )
 
     def make_maps():
         for from_y in range(2):
@@ -528,18 +575,11 @@
             )
 
     def prepare(idx, term):
-        lap, slope = along_depth(idx)
-        partial = term + speed_sq[...].reshape(rows, depth) * (
-            SECOND_COEFFS[1] * lap - slopes[2].reshape(rows, depth) * slope
-        )
-        base[...] = partial.reshape(n_i, n_x, depth)
+        base[...] = term.reshape(n_i, n_x, depth) + speed_sq[...] * bare(idx)
 
     def interior(now, other, i):
-        lap, slope_i, slope_x = across(now, i)
-        center = field[now, i + 4, inner_x, :]
-        change = base[i] + speed_sq[i] * (
-            3.0 * SECOND_COEFFS[0] * center + lap - slopes[0, i] * slope_i - slopes[1, i] * slope_x
-        )
+        center, sideways = lateral(now, i)
+        change = base[i] + speed_sq[i] * sideways
         field[other, i + 4, inner_x, :] = 2.0 * center - field[other, i + 4, inner_x, :] + change
         return center, change
 
@@ -582,41 +622,63 @@
         predicted = jnp.sum(picked * row_map[...], axis=0, keepdims=True)
         residual_ref[t] = predicted
 
+    def adjoint_start(part):
+        @pl.loop(part * middle, (part + 1) * middle)
+        def _(i):
+            center, sideways = lateral(2, i)
+            field[3, i + 4, inner_x, :] = (
+                2.0 * center - field[3, i + 4, inner_x, :] + speed_sq[i] * (adj_base[i] + sideways)
+            )
+
+    def task_now():
+        tile_start(ADJ_NOW)
+        make_maps()
+
+    def task_before():
+        tile_start(ADJ_BEFORE)
+
+    def task_traces():
+        @pl.loop(1, n_group)
+        def _(r):
+            obs_copy(lax.rem(me + r, n_group), me).start()
+
+    def task_halos():
+        tile_finish(ADJ_NOW)
+        for part in halves:
+            stage(2, part)
+            send(2, part)
+        adj_base[...] = bare(2)
+
+    def task_upper():
+        tile_finish(ADJ_BEFORE)
+        adjoint_start(0)
+
+    def task_lower():
+        adjoint_start(1)
+
+    tasks = [task_now, task_before, task_traces, task_halos, task_upper, task_lower, make_traces]
+    times = [1 + n * (steps - 2) // (len(tasks) - 1) for n in range(len(tasks))]
+
     @pl.loop(0, steps)
     def _(t):
         now = lax.rem(t, 2)
         other = 1 - now
-        high, low = split_bf16(src_rows * wavelet[pl.ds(t, 1), :])
-        prepare(now, dot_nt(high, src_cols) + dot_nt(low, src_cols))
-
-        @pl.loop(0, n_i)
-        def _(i):
-            _, change = interior(now, other, i)
-            accel[t, i] = change
-
-        @pl.when(t == 1)
-        def _():
-            tile_start(ADJ_NOW)
-            make_maps()
-
-        @pl.when(t == 4)
-        def _():
-            make_traces()
-
-        @pl.when(t == 3)
-        def _():
-            tile_start(ADJ_BEFORE)
+
+        @pl.when(t > 0)
+        def _():
+            prepare(now, inject_sources(t))
+
+            @pl.loop(0, n_i)
+            def _(i):
+                _, change = interior(now, other, i)
+                accel[t, i] = change
+
+        for at, task in zip(times, tasks):
+            pl.when(t == at)(task)
 
         @pl.when(t >= 1)
         def _():
             sample(now, t - 1)
-
-        @pl.when(t == steps - 1)
-        def _():
-            tile_finish(ADJ_NOW)
-            for part in halves:
-                stage(2, part)
-                send(2, part)
 
         for part in halves:
             finish(now, part)
@@ -627,7 +689,6 @@
                 send(other, part)
 
     sample(steps % 2, steps - 1)
-    tile_finish(ADJ_BEFORE)
 
     @pl.loop(0, steps)
     def _(j):
@@ -635,12 +696,20 @@
         other = 5 - now
         t = steps - 1 - j
         high, low = split_bf16(row_map[...] * (residual_ref[t] - traces[pl.ds(t, 1), :]))
-        prepare(now, dot_nt(high, zmap_t[...]) + dot_nt(low, zmap_t[...]))
-
-        @pl.loop(0, n_i)
-        def _(i):
-            center, _ = interior(now, other, i)
-            image[i] += center * accel[t + 1, i]
+        injected = dot_nt(high, zmap_t[...]) + dot_nt(low, zmap_t[...])
+
+        @pl.when(j == 0)
+        def _():
+            field[3, inner_i, inner_x, :] += injected.reshape(n_i, n_x, depth)
+
+        @pl.when(j > 0)
+        def _():
+            prepare(now, injected)
+
+            @pl.loop(0, n_i)
+            def _(i):
+                center, _ = interior(now, other, i)
+                image[i] += center * accel[t + 1, i]
 
         @pl.when(j == steps - 1)
         def _():
@@ -668,25 +737,40 @@
     home_finish(1)
 
 
-def hand_over(*arrays):
-    count = len(arrays)
-
-    def kernel(*refs):
+def finish_kernel(shape, slabs, last, previous):
+    dz, tile_i, full_x = shape
+    _, n_groups, _, lanes = slabs.shape
+    group = lanes // dz
+
+    def kernel(slabs_in, last_in, previous_in, gradient, last_out, previous_out, sem):
         copies = [
-            pltpu.make_async_copy(refs[n], refs[count + n], refs[2 * count].at[n]) for n in range(count)
+            pltpu.make_async_copy(last_in, last_out, sem.at[0]),
+            pltpu.make_async_copy(previous_in, previous_out, sem.at[1]),
         ]
         for copy in copies:
             copy.start()
+        far = (
+            lax.broadcasted_iota(jnp.int32, (full_x, full_x), 0) - lax.broadcasted_iota(jnp.int32, (full_x, full_x), 1)
+        ).astype(jnp.float32)
+        weights = jnp.exp(-jnp.abs(far) / SMOOTH)
+        weights = weights / jnp.sum(weights, axis=0, keepdims=True)
+        for a in range(2):
+            for ig in range(n_groups):
+                lines = dot_tn_exact(slabs_in[a, ig], weights)
+                for j in range(group):
+                    gradient[:, (a * n_groups + ig) * group + j, :] = lines[j * dz:(j + 1) * dz]
         for copy in copies:
             copy.wait()
 
+    vmem = pl.BlockSpec(memory_space=pltpu.VMEM)
+    anywhere = pl.BlockSpec(memory_space=pl.ANY)
     return pl.pallas_call(
         kernel,
-        out_shape=[jax.ShapeDtypeStruct(array.shape, array.dtype) for array in arrays],
-        in_specs=[pl.BlockSpec(memory_space=pltpu.VMEM)] * count,
-        out_specs=[pl.BlockSpec(memory_space=pl.ANY)] * count,
-        scratch_shapes=[pltpu.SemaphoreType.DMA((count,))],
-    )(*arrays)
+        out_shape=[jax.ShapeDtypeStruct(dims, jnp.float32) for dims in (shape, last.shape, previous.shape)],
+        in_specs=[vmem] * 3,
+        out_specs=[vmem, anywhere, anywhere],
+        scratch_shapes=[pltpu.SemaphoreType.DMA((2,))],
+    )(slabs, last, previous)
 
 
 def per_device(
@@ -710,11 +794,9 @@
     anywhere = pl.BlockSpec(memory_space=pl.ANY)
     dma = pltpu.SemaphoreType.DMA
     kernel = functools.partial(wave_kernel, (tile_i, tile_x, n_i, n_x, depth, steps, n_xline, fused))
-    grad_shape = (dz, tile_i, full_x) if fused else block
-    if fused:
-        g_shapes = (n_xline, n_i // group, n_x, 128), (2, n_i // group, full_x, 128), (full_x, full_x)
-    else:
-        g_shapes = ((8, 128),) * 3
+    grad_shape = (2, n_i // group, full_x, 128) if fused else block
+    slab_shape = (n_xline, n_i // group, n_x, 128) if fused else (8, 128)
+    small_shapes = [observed, rec_cells, rec_counts, src_cell[None, :], wavelet]
     raw, last, previous = pl.pallas_call(
         kernel,
         out_shape=[
@@ -722,15 +804,15 @@
             jax.ShapeDtypeStruct(fwd_now.shape, jnp.float32),
             jax.ShapeDtypeStruct(fwd_now.shape, jnp.float32),
         ],
-        in_specs=[anywhere] * 6 + [vmem] * 5,
-        out_specs=[vmem, anywhere, anywhere],
+        in_specs=[anywhere] * 11,
+        out_specs=[anywhere if fused else vmem, anywhere, anywhere],
         scratch_shapes=[
             pltpu.VMEM((5, n_i + 8, n_x + 16, depth), jnp.float32),
             pltpu.VMEM(block, jnp.float32),
             pltpu.VMEM((5, 2, n_i, 4, depth), jnp.float32),
             pltpu.VMEM((5, 2, n_i, 4, depth), jnp.float32),
             pltpu.VMEM((5, 2, 4, n_x, depth), jnp.float32),
-            pltpu.VMEM((steps + 1,) + block, jnp.float32),
+            pltpu.VMEM((steps,) + block, jnp.float32),
             pltpu.VMEM(block, jnp.float32),
             pltpu.VMEM(block, jnp.float32),
             pltpu.VMEM((3,) + block, jnp.float32),
@@ -744,25 +826,25 @@
             pltpu.VMEM((8, slots), jnp.int32),
             pltpu.VMEM((2, 8, slots), jnp.int32),
             pltpu.VMEM((n_group,) + observed.shape, jnp.float32),
-            pltpu.VMEM(g_shapes[0], jnp.float32),
-            pltpu.VMEM(g_shapes[1], jnp.float32),
-            pltpu.VMEM(g_shapes[2], jnp.float32),
+            pltpu.VMEM(slab_shape, jnp.float32),
+            *[pltpu.VMEM(value.shape, value.dtype) for value in small_shapes],
+            pltpu.VMEM(block, jnp.float32),
             dma((5, 6)), dma((5, 6)),
             dma((6, 2)), dma((6, 2)), dma((6,)),
             dma((2,)), dma((2,)),
             dma((n_group,)), dma((n_group,)),
             dma((2, 2)), dma((2, 2)), dma((2,)),
-            dma((n_xline,)), dma((2, n_xline // 2)),
+            dma((n_xline,)), dma((2, n_xline // 2)), dma((1,)), dma((5,)),
         ],
         compiler_params=pltpu.CompilerParams(
             collective_id=0, has_side_effects=True, vmem_limit_bytes=56 * 1024 * 1024
         ),
     )(
         log_density, fwd_now, velocity, fwd_before, adj_now, adj_before,
-        observed, rec_cells, rec_counts, src_cell[None, :], wavelet,
+        *small_shapes,
     )
     if fused:
-        return hand_over(raw, last, previous)
+        return finish_kernel((dz, tile_i, full_x), raw, last, previous)
 
     places = []
     for xl in range(n_xline):
@@ -782,7 +864,7 @@
         "phixz,ypx->zhiy", columns, weights.reshape(full_x, n_xline // 2, n_x),
         precision=lax.Precision.HIGHEST,
     ).reshape(dz, tile_i, full_x)
-    return (gradient,) + tuple(hand_over(last, previous))
+    return gradient, last, previous
 
 
 def solution(mesh):

time: 83.8 us -> 79.6 us (0.950)
  Pallas kernels: 81.9 us -> 77.8 us
    pallas_call x1, Pallas kernels: 79.7 us -> 75.1 us  [per_device(): pl.pallas_call(kernel, out_shape=[jax.ShapeDtypeStruct(grad_shape, jnp.fl...]
where the time goes in v3:
time: 79.6 us; the launch traced here: 78.4 us
  Pallas kernels  77.8 us (98%)
    pallas_call x1, Pallas kernels, per_device(): pl.pallas_call(kernel, out_shape=[jax.ShapeDtypeStruct(grad_shape, jnp.fl...  75.1 us
    pallas_call x1, Pallas kernels, finish_kernel(): pl.pallas_call(kernel, out_shape=[jax.ShapeDtypeStruct(dims, jnp.float32)...  2.71 us

profile of v3, /device:TPU:0, one launch (start us, length us, event | category | flops | bytes accessed | tf_op | source)
XLA Modules:
  0.0 78.4 jit_solution(4052818924209932850)
XLA Ops:
  0.6 75.1 %shard_map.130 = (f32[2,4,64,128]{3,2,1,0:T(8,128)}, f32[32,8,256]{2,1,0:T(8,128)}, f32[32,8,256]{2,1,0:T(8,128)}) custom-call(f32[32,8,256]{2,1,0:T(8,128)} %log_density.1, f32[32,8,256]{2,1,0:T(8,128)} %fwd_now.1, f32[32,8,256]{2,1,0:T(8,128)} %velocity.1, f32[32,8,256]{2,1,0:T(8,128)} %fwd_before.1, f32[32,8,256]{2,1,0:T(8,128)} %adj_now.1, ...), custom_call_target="tpu_custom_call" | custom-call | tf_op jit(solution)/shard_map/pallas_call | solution.py:800
  75.7 2.7 %shard_map.131 = (f32[32,32,64]{2,1,0:T(8,128)}, f32[32,8,256]{2,1,0:T(8,128)}, f32[32,8,256]{2,1,0:T(8,128)}) custom-call(f32[2,4,64,128]{3,2,1,0:T(8,128)} %get-tuple-element.6.slabs_in, f32[32,8,256]{2,1,0:T(8,128)} %get-tuple-element.7.last_in, f32[32,8,256]{2,1,0:T(8,128)} %get-tuple-element.8.previous_in), custom_call_target="tpu_custom_call" | custom-call | tf_op jit(solution)/shard_map/pallas_call | solution.py:767

commit v4 on v3

--- a/solution.py
+++ b/solution.py
@@ -57,8 +57,8 @@
     grad_out, last_out, previous_out,
     field, vel, x_in, x_out, i_in, accel, base, image, slopes, speed_sq, wx,
     row_map, zmap_t, z_mat, residual_ref, traces, list_out, list_in, obs_in, g_send,
-    held_observed, held_cells, held_counts, held_src, held_wavelet, adj_base,
-    send_sem, recv_sem, rt_send, rt_recv, rt_local, list_send, list_recv, obs_send, obs_recv,
+    held_observed, held_cells, held_counts, held_src, held_wavelet, row_mat, wide, deep,
+    x_send, x_recv, i_send, i_recv, rt_send, rt_recv, rt_local, list_send, list_recv, obs_send, obs_recv,
     ret_send, ret_recv, ret_local, g_ssem, g_rsem, g_local, small_sem,
 ):
     tile_i, tile_x, n_i, n_x, depth, steps, n_xline, fused = sizes
@@ -120,21 +120,26 @@
         copy.start()
     observed, rec_cells, rec_counts, src_cell, wavelet = small_held
 
-    def beside(idx, way, part):
+    layers = depth // 128
+    half_x = n_x // 2
+
+    def beside(idx, way, part, d):
         part_rows = pl.ds(part * middle, middle)
-        sem = way + 4 * part
-        return pltpu.make_async_remote_copy(
-            src_ref=x_out.at[idx, way, part_rows], dst_ref=x_in.at[idx, 1 - way, part_rows],
-            send_sem=send_sem.at[idx, sem], recv_sem=recv_sem.at[idx, sem],
+        return pltpu.make_async_remote_copy(
+            src_ref=x_out.at[idx, way, d, part_rows], dst_ref=x_in.at[idx, 1 - way, d, part_rows],
+            send_sem=x_send.at[idx, way, part, d], recv_sem=x_recv.at[idx, way, part, d],
             device_id=target[way], device_id_type=MESH,
         )
 
-    def above(idx, part, side):
+    def above(idx, part, c, d, arriving):
         up = part == 0
         return pltpu.make_async_remote_copy(
-            src_ref=field.at[idx, pl.ds(4 + part * (n_i - 4), 4), inner_x, :],
-            dst_ref=i_in.at[idx, part if side else 1 - part],
-            send_sem=send_sem.at[idx, 2 + part], recv_sem=recv_sem.at[idx, 3 - part if side else 2 + part],
+            src_ref=field.at[
+                idx, pl.ds(4 + part * (n_i - 4), 4), pl.ds(8 + c * half_x, half_x), pl.ds(d * 128, 128)
+            ],
+            dst_ref=i_in.at[idx, part if arriving else 1 - part, d, c],
+            send_sem=i_send.at[idx, part, c, d],
+            recv_sem=i_recv.at[idx, 1 - part if arriving else part, c, d],
             device_id={
                 "xline": jnp.where(up, target[UP]["xline"], target[DOWN]["xline"]), "inline": other_core
             },
@@ -144,35 +149,36 @@
     def has_row(part):
         return jnp.where(part == 0, q, 3 - q) > 0
 
-    def send(idx, part):
-        for way in (LEFT, RIGHT):
-            @pl.when(has[way])
-            def _():
-                beside(idx, way, part).start()
+    def send(idx, part, d, c):
+        @pl.when(has[c])
+        def _():
+            beside(idx, c, part, d).start()
 
         @pl.when(has_row(part))
         def _():
-            above(idx, part, False).start()
-
-    def stage(idx, part):
-        part_rows = pl.ds(part * middle, middle)
-        field_rows = pl.ds(4 + part * middle, middle)
-        x_out[idx, 0, part_rows] = field[idx, field_rows, pl.ds(8, 4), :]
-        x_out[idx, 1, part_rows] = field[idx, field_rows, pl.ds(4 + n_x, 4), :]
-
-    def finish(idx, part):
-        for way in (LEFT, RIGHT):
-            @pl.when(has[way])
-            def _():
-                beside(idx, way, part).wait_send()
-                beside(idx, 1 - way, part).wait_recv()
+            above(idx, part, c, d, False).start()
+
+    def finish(idx, part, d, c):
+        @pl.when(has[c])
+        def _():
+            beside(idx, c, part, d).wait_send()
+            beside(idx, 1 - c, part, d).wait_recv()
 
         @pl.when(has_row(part))
         def _():
-            above(idx, part, False).wait_send()
-            above(idx, part, True).wait_recv()
+            above(idx, part, c, d, False).wait_send()
+            above(idx, part, c, d, True).wait_recv()
+
+    def send_all(idx):
+        for part, d, c in pieces:
+            rows_at = pl.ds(part * middle, middle)
+            x_out[idx, c, d, rows_at] = field[
+                idx, pl.ds(4 + part * middle, middle), pl.ds(8 + c * (n_x - 4), 4), pl.ds(d * 128, 128)
+            ]
+            send(idx, part, d, c)
 
     halves = (1 - y, y)
+    pieces = [(part, d, c) for part in halves for d in range(layers) for c in range(2)]
 
     sources = (log_density, fwd_now, velocity, fwd_before, adj_now, adj_before)
     places = (DENSITY, 0, None, 1, 2, 3)
@@ -430,6 +436,21 @@
     z_mat[:, pl.ds(0, depth)] = second.astype(jnp.bfloat16)
     z_mat[:, pl.ds(depth, depth)] = first.astype(jnp.bfloat16)
 
+    at = lax.broadcasted_iota(jnp.int32, (rows, rows), 0)
+    to = lax.broadcasted_iota(jnp.int32, (rows, rows), 1)
+    step_i = div(to, n_x) - div(at, n_x)
+    step_x = mod(to, n_x) - mod(at, n_x)
+    lateral_lap = jnp.zeros((rows, rows), jnp.float32)
+    for n, (along, still) in enumerate(((step_i, step_x), (step_x, step_i))):
+        along = jnp.where(still == 0, along, 0)
+        first = jnp.zeros((rows, rows), jnp.float32)
+        for k in range(1, 5):
+            lateral_lap = jnp.where((along == k) | (along == -k), SECOND_COEFFS[k] / SECOND_COEFFS[1], lateral_lap)
+            first = jnp.where(along == k, FIRST_COEFFS[k - 1] / FIRST_COEFFS[0], first)
+            first = jnp.where(along == -k, -FIRST_COEFFS[k - 1] / FIRST_COEFFS[0], first)
+        row_mat[pl.ds((n + 1) * rows, rows), :] = first.astype(jnp.bfloat16)
+    row_mat[pl.ds(0, rows), :] = lateral_lap.astype(jnp.bfloat16)
+
     full_x = tile_x * n_xline
     cells = src_cell[...]
     src_i = div(cells, full_x * depth) - q * n_i
@@ -443,10 +464,22 @@
     def flat(idx):
         return field[idx, inner_i, inner_x, :].reshape(rows, depth)
 
-    def along_depth(idx):
+    def differences(idx):
         high, low = split_bf16(flat(idx))
-        both = dot(high, z_mat[...]) + dot(low, z_mat[...])
-        return both[:, :depth], both[:, depth:]
+        wide[...] = dot(row_mat[...], high) + dot(row_mat[...], low)
+        deep[...] = dot(high, z_mat[...]) + dot(low, z_mat[...])
+
+    def operator(idx, i):
+        def line(n):
+            return pl.ds(pl.multiple_of(n * rows + i * n_x, n_x), n_x)
+
+        center = field[idx, i + 4, inner_x, :]
+        return center, (
+            3.0 * SECOND_COEFFS[0] * center
+            + SECOND_COEFFS[1] * (wide[line(0), :] + deep[line(0), pl.ds(0, depth)])
+            - slopes[0, i] * wide[line(1), :] - slopes[1, i] * wide[line(2), :]
+            - slopes[2, i] * deep[line(0), pl.ds(depth, depth)]
+        )
 
     def across(idx, i):
         lap = slope_i = slope_x = None
@@ -467,50 +500,35 @@
         return lap, slope_i, slope_x
 
     tile_finish(RHO)
-    for part in halves:
-        stage(DENSITY, part)
-        send(DENSITY, part)
+    send_all(DENSITY)
     tile_finish(NOW)
-    for part in halves:
-        stage(0, part)
-        send(0, part)
-
-    slopes[2] = (FIRST_COEFFS[0] * FIRST_COEFFS[0] * along_depth(DENSITY)[1]).reshape(n_i, n_x, depth)
-
-    def bare(idx):
-        lap, slope = along_depth(idx)
-        return (SECOND_COEFFS[1] * lap - slopes[2].reshape(rows, depth) * slope).reshape(n_i, n_x, depth)
+    send_all(0)
+
+    high, low = split_bf16(flat(DENSITY))
+    deep[...] = dot(high, z_mat[...]) + dot(low, z_mat[...])
+    slopes[2] = ((FIRST_COEFFS[0] * FIRST_COEFFS[0]) * deep[:, pl.ds(depth, depth)]).reshape(n_i, n_x, depth)
+    differences(0)
 
     def inject_sources(t):
         high, low = split_bf16(src_rows * wavelet[pl.ds(t, 1), :])
         return dot_nt(high, src_cols) + dot_nt(low, src_cols)
 
-    base[...] = bare(0)
     accel[0] = inject_sources(0).reshape(n_i, n_x, depth)
 
-    finish(DENSITY, 0)
-    finish(DENSITY, 1)
-    field[DENSITY, pl.ds(0, 4), inner_x, :] = i_in[DENSITY, 0]
-    field[DENSITY, pl.ds(n_i + 4, 4), inner_x, :] = i_in[DENSITY, 1]
-    field[DENSITY, inner_i, pl.ds(4, 4), :] = x_in[DENSITY, 0]
-    field[DENSITY, inner_i, pl.ds(8 + n_x, 4), :] = x_in[DENSITY, 1]
-
-    def lateral(idx, i):
-        lap, slope_i, slope_x = across(idx, i)
-        center = field[idx, i + 4, inner_x, :]
-        return center, (
-            3.0 * SECOND_COEFFS[0] * center + lap - slopes[0, i] * slope_i - slopes[1, i] * slope_x
-        )
+    for part, d, c in pieces:
+        finish(DENSITY, part, d, c)
+    for d in range(layers):
+        lanes = pl.ds(d * 128, 128)
+        for side in range(2):
+            for c in range(2):
+                field[DENSITY, pl.ds(side * (n_i + 4), 4), pl.ds(8 + c * half_x, half_x), lanes] = i_in[DENSITY, side, d, c]
+            field[DENSITY, inner_i, pl.ds(4 + side * (n_x + 4), 4), lanes] = x_in[DENSITY, side, d]
 
     @pl.loop(0, n_i)
     def _(i):
         _, slope_i, slope_x = across(DENSITY, i)
-        slopes[0, i] = slope_i
-        slopes[1, i] = slope_x
-
-    @pl.loop(0, n_i)
-    def _(i):
-        base[i] += lateral(0, i)[1]
+        slopes[0, i] = FIRST_COEFFS[0] * slope_i
+        slopes[1, i] = FIRST_COEFFS[0] * slope_x
 
     tile_finish(SPEED)
     column = lax.broadcasted_iota(jnp.int32, (n_x, depth), 0)
@@ -519,11 +537,13 @@
     def _(i):
         square = vel[i] * vel[i]
         speed_sq[i] = square
-        accel[0, i] += square * base[i]
+        accel[0, i] += square * operator(0, i)[1]
         for k in range(1, 5):
             weight = jnp.where(
-                column < k, SECOND_COEFFS[k] + FIRST_COEFFS[k - 1] * slopes[1, i],
-                jnp.where(column >= n_x - k, SECOND_COEFFS[k] - FIRST_COEFFS[k - 1] * slopes[1, i], 0.0),
+                column < k, SECOND_COEFFS[k] + (FIRST_COEFFS[k - 1] / FIRST_COEFFS[0]) * slopes[1, i],
+                jnp.where(
+                    column >= n_x - k, SECOND_COEFFS[k] - (FIRST_COEFFS[k - 1] / FIRST_COEFFS[0]) * slopes[1, i], 0.0
+                ),
             )
             wx[k - 1, i] = square * weight
 
@@ -575,46 +595,40 @@
             )
 
     def prepare(idx, term):
-        base[...] = term.reshape(n_i, n_x, depth) + speed_sq[...] * bare(idx)
+        base[...] = term.reshape(n_i, n_x, depth)
+        differences(idx)
 
     def interior(now, other, i):
-        center, sideways = lateral(now, i)
-        change = base[i] + speed_sq[i] * sideways
+        center, value = operator(now, i)
+        change = base[i] + speed_sq[i] * value
         field[other, i + 4, inner_x, :] = 2.0 * center - field[other, i + 4, inner_x, :] + change
         return center, change
 
-    def correction(now, i):
-        pair = jnp.concatenate([x_in[now, 1, i], x_in[now, 0, i]], axis=0)
-        total = None
-        for k in range(1, 5):
-            pieces = [pltpu.roll(pair, k, axis=0)]
-            if n_x > 16:
-                pieces.append(jnp.zeros((n_x - 16, depth), jnp.float32))
-            pieces.append(pltpu.roll(pair, 8 - k, axis=0))
-            term = wx[k - 1, i] * jnp.concatenate(pieces, axis=0)
-            total = term if total is None else total + term
-        return total
-
-    def correct(now, other, part, t):
+    def correct(now, other, part, d, c, t):
         up = part == 0
         sign = jnp.where(up, 1.0, -1.0)
+        columns, lanes = pl.ds(c * half_x, half_x), pl.ds(d * 128, 128)
         for r in range(middle):
             i = jnp.where(up, r, n_i - 1 - r)
-            change = correction(now, i)
+            halo = x_in[now, c, d, i]
+            pair = jnp.concatenate([halo] * (half_x // 4), axis=0)
+            change = wx[3, i, columns, lanes] * pair
+            for k in range(1, 4):
+                change += wx[k - 1, i, columns, lanes] * pltpu.roll(pair, half_x - k if c else k, axis=0)
             lap = None
             for h in range(4 - r):
                 k = r + 1 + h
-                halo = i_in[now, part, jnp.where(up, 3 - h, h)]
-                terms = SECOND_COEFFS[k] * halo, FIRST_COEFFS[k - 1] * halo
+                halo = i_in[now, part, d, c, jnp.where(up, 3 - h, h)]
+                terms = SECOND_COEFFS[k] * halo, (FIRST_COEFFS[k - 1] / FIRST_COEFFS[0]) * halo
                 lap, slope = terms if lap is None else (lap + terms[0], slope + terms[1])
             if lap is not None:
-                change = change + speed_sq[i] * (lap + (sign * slopes[0, i]) * slope)
-            fresh = field[other, i + 4, inner_x, :] + change
-            field[other, i + 4, inner_x, :] = fresh
-            x_out[other, 0, i] = fresh[:4]
-            x_out[other, 1, i] = fresh[n_x - 4:]
+                change += speed_sq[i, columns, lanes] * (lap + (sign * slopes[0, i, columns, lanes]) * slope)
+            spot = (other, i + 4, pl.ds(8 + c * half_x, half_x), lanes)
+            fresh = field[spot] + change
+            field[spot] = fresh
+            x_out[other, c, d, i] = fresh[half_x - 4:] if c else fresh[:4]
             if t is not None:
-                accel[t, i] += change
+                accel[t, i, columns, lanes] += change
 
     def sample(idx, t):
         high, low = split_bf16(flat(idx))
@@ -622,14 +636,6 @@
         predicted = jnp.sum(picked * row_map[...], axis=0, keepdims=True)
         residual_ref[t] = predicted
 
-    def adjoint_start(part):
-        @pl.loop(part * middle, (part + 1) * middle)
-        def _(i):
-            center, sideways = lateral(2, i)
-            field[3, i + 4, inner_x, :] = (
-                2.0 * center - field[3, i + 4, inner_x, :] + speed_sq[i] * (adj_base[i] + sideways)
-            )
-
     def task_now():
         tile_start(ADJ_NOW)
         make_maps()
@@ -644,20 +650,21 @@
 
     def task_halos():
         tile_finish(ADJ_NOW)
-        for part in halves:
-            stage(2, part)
-            send(2, part)
-        adj_base[...] = bare(2)
-
-    def task_upper():
+        send_all(2)
+
+    def task_adjoint():
         tile_finish(ADJ_BEFORE)
-        adjoint_start(0)
-
-    def task_lower():
-        adjoint_start(1)
-
-    tasks = [task_now, task_before, task_traces, task_halos, task_upper, task_lower, make_traces]
-    times = [1 + n * (steps - 2) // (len(tasks) - 1) for n in range(len(tasks))]
+        differences(2)
+
+        @pl.loop(0, n_i, unroll=2)
+        def _(i):
+            center, value = operator(2, i)
+            field[3, i + 4, inner_x, :] = (
+                2.0 * center - field[3, i + 4, inner_x, :] + speed_sq[i] * value
+            )
+
+    tasks = [task_now, task_before, task_traces, task_halos, task_adjoint, make_traces]
+    times = [1 + n * (steps - 2) // len(tasks) for n in range(len(tasks))]
 
     @pl.loop(0, steps)
     def _(t):
@@ -668,7 +675,7 @@
         def _():
             prepare(now, inject_sources(t))
 
-            @pl.loop(0, n_i)
+            @pl.loop(0, n_i, unroll=2)
             def _(i):
                 _, change = interior(now, other, i)
                 accel[t, i] = change
@@ -680,13 +687,13 @@
         def _():
             sample(now, t - 1)
 
-        for part in halves:
-            finish(now, part)
-            correct(now, other, part, t)
+        for part, d, c in pieces:
+            finish(now, part, d, c)
+            correct(now, other, part, d, c, t)
 
             @pl.when(t < steps - 1)
             def _():
-                send(other, part)
+                send(other, part, d, c)
 
     sample(steps % 2, steps - 1)
 
@@ -706,7 +713,7 @@
         def _():
             prepare(now, injected)
 
-            @pl.loop(0, n_i)
+            @pl.loop(0, n_i, unroll=2)
             def _(i):
                 center, _ = interior(now, other, i)
                 image[i] += center * accel[t + 1, i]
@@ -715,13 +722,13 @@
         def _():
             home_start(0)
 
-        for part in halves:
-            finish(now, part)
-            correct(now, other, part, None)
+        for part, d, c in pieces:
+            finish(now, part, d, c)
+            correct(now, other, part, d, c, None)
 
             @pl.when(j < steps - 1)
             def _():
-                send(other, part)
+                send(other, part, d, c)
 
     @pl.loop(0, n_i)
     def _(i):
@@ -788,6 +795,7 @@
     dz = depth // n_xline
     fused = dz >= 8 and 128 % dz == 0 and depth % 128 == 0 and n_i % (128 // dz) == 0
     group = 128 // dz if fused else 1
+    layers = depth // 128
 
     block = (n_i, n_x, depth)
     vmem = pl.BlockSpec(memory_space=pltpu.VMEM)
@@ -809,9 +817,9 @@
         scratch_shapes=[
             pltpu.VMEM((5, n_i + 8, n_x + 16, depth), jnp.float32),
             pltpu.VMEM(block, jnp.float32),
-            pltpu.VMEM((5, 2, n_i, 4, depth), jnp.float32),
-            pltpu.VMEM((5, 2, n_i, 4, depth), jnp.float32),
-            pltpu.VMEM((5, 2, 4, n_x, depth), jnp.float32),
+            pltpu.VMEM((5, 2, layers, n_i, 4, 128), jnp.float32),
+            pltpu.VMEM((5, 2, layers, n_i, 4, 128), jnp.float32),
+            pltpu.VMEM((5, 2, layers, 2, 4, tile_x, 128), jnp.float32),
             pltpu.VMEM((steps,) + block, jnp.float32),
             pltpu.VMEM(block, jnp.float32),
             pltpu.VMEM(block, jnp.float32),
@@ -828,8 +836,10 @@
             pltpu.VMEM((n_group,) + observed.shape, jnp.float32),
             pltpu.VMEM(slab_shape, jnp.float32),
             *[pltpu.VMEM(value.shape, value.dtype) for value in small_shapes],
-            pltpu.VMEM(block, jnp.float32),
-            dma((5, 6)), dma((5, 6)),
+            pltpu.VMEM((3 * rows, rows), jnp.bfloat16),
+            pltpu.VMEM((3 * rows, depth), jnp.float32),
+            pltpu.VMEM((rows, 2 * depth), jnp.float32),
+            *[dma((5, 2, 2, layers)) for _ in range(4)],
             dma((6, 2)), dma((6, 2)), dma((6,)),
             dma((2,)), dma((2,)),
             dma((n_group,)), dma((n_group,)),

time: 79.6 us -> 76.6 us (0.962); the launches traced: 78.4 us -> 76.4 us
  Pallas kernels: 77.8 us -> 75.8 us
    pallas_call x1, Pallas kernels: 75.1 us -> 73 us  [per_device(): pl.pallas_call(kernel, out_shape=[jax.ShapeDtypeStruct(grad_shape, jnp.fl...]
where the time goes in v4:
time: 76.6 us; the launch traced here: 76.4 us
  Pallas kernels  75.8 us (99%)
    pallas_call x1, Pallas kernels, per_device(): pl.pallas_call(kernel, out_shape=[jax.ShapeDtypeStruct(grad_shape, jnp.fl...  73 us
    pallas_call x1, Pallas kernels, finish_kernel(): pl.pallas_call(kernel, out_shape=[jax.ShapeDtypeStruct(dims, jnp.float32)...  2.71 us

profile of v4, /device:TPU:0, one launch (start us, length us, event | category | flops | bytes accessed | tf_op | source)
XLA Modules:
  0.0 76.4 jit_solution(16176878242409026444)
XLA Ops:
  0.6 73.0 %shard_map.130 = (f32[2,4,64,128]{3,2,1,0:T(8,128)}, f32[32,8,256]{2,1,0:T(8,128)}, f32[32,8,256]{2,1,0:T(8,128)}) custom-call(f32[32,8,256]{2,1,0:T(8,128)} %log_density.1, f32[32,8,256]{2,1,0:T(8,128)} %fwd_now.1, f32[32,8,256]{2,1,0:T(8,128)} %velocity.1, f32[32,8,256]{2,1,0:T(8,128)} %fwd_before.1, f32[32,8,256]{2,1,0:T(8,128)} %adj_now.1, ...), custom_call_target="tpu_custom_call" | custom-call | tf_op jit(solution)/shard_map/pallas_call | solution.py:808
  73.7 2.7 %shard_map.131 = (f32[32,32,64]{2,1,0:T(8,128)}, f32[32,8,256]{2,1,0:T(8,128)}, f32[32,8,256]{2,1,0:T(8,128)}) custom-call(f32[2,4,64,128]{3,2,1,0:T(8,128)} %get-tuple-element.6.slabs_in, f32[32,8,256]{2,1,0:T(8,128)} %get-tuple-element.7.last_in, f32[32,8,256]{2,1,0:T(8,128)} %get-tuple-element.8.previous_in), custom_call_target="tpu_custom_call" | custom-call | tf_op jit(solution)/shard_map/pallas_call | solution.py:774

commit v5 on v4

--- a/solution.py
+++ b/solution.py
@@ -59,7 +59,7 @@
     row_map, zmap_t, z_mat, residual_ref, traces, list_out, list_in, obs_in, g_send,
     held_observed, held_cells, held_counts, held_src, held_wavelet, row_mat, wide, deep,
     x_send, x_recv, i_send, i_recv, rt_send, rt_recv, rt_local, list_send, list_recv, obs_send, obs_recv,
-    ret_send, ret_recv, ret_local, g_ssem, g_rsem, g_local, small_sem,
+    ret_send, ret_recv, ret_local, g_ssem, g_rsem, g_local, small_sem, pass_send, pass_recv,
 ):
     tile_i, tile_x, n_i, n_x, depth, steps, n_xline, fused = sizes
     rows = n_i * n_x
@@ -80,6 +80,8 @@
     stays = y == core
     has = (xl >= 2, xl < n_xline - 2, q > 0, q < 3)
     other_core = 1 - core
+    shot = lax.axis_index("shots")
+    shares = (RHO, SPEED) if lax.axis_size("shots") == 2 else ()
     target = (
         {"xline": xl - 2, "inline": other_core},
         {"xline": xl + 2, "inline": other_core},
@@ -111,6 +113,9 @@
             peer = lax.rem(me + r, n_group)
             greet({"xline": peer // 2, "inline": lax.rem(peer, 2)})
         greeted = n_group - 1
+    if shares:
+        greet({"shots": 1 - shot})
+        greeted = greeted + 1
 
     small = [
         pltpu.make_async_copy(given, held, small_sem.at[n])
@@ -217,9 +222,15 @@
 
     def tile_start(n):
         for a in range(2):
-            @pl.when(leaves(a))
+            @pl.when(jnp.logical_and(stays, cp != a) if n in shares else leaves(a))
             def _():
                 tile_copy(n, a).start()
+
+        if n in shares:
+            for a in range(2):
+                @pl.when(jnp.logical_not(stays))
+                def _():
+                    half_copy(n, a).start()
 
         @pl.when(stays)
         def _():
@@ -227,17 +238,61 @@
 
     def tile_finish(n):
         for from_y in range(2):
-            @pl.when(arrives(from_y))
+            @pl.when(jnp.logical_and(arrives(from_y), y == from_y) if n in shares else arrives(from_y))
             def _():
                 tile_arrival(n, from_y).wait_recv()
         for a in range(2):
-            @pl.when(leaves(a))
+            @pl.when(jnp.logical_and(stays, cp != a) if n in shares else leaves(a))
             def _():
                 tile_copy(n, a).wait_send()
 
         @pl.when(stays)
         def _():
             own_copy(n).wait()
+
+        if n in shares:
+            for a in range(2):
+                @pl.when(jnp.logical_not(stays))
+                def _():
+                    half_copy(n, a).wait_send()
+            pass_on(n).wait_send()
+            passed_on(n).wait_recv()
+
+    def half_landing(n, from_y, which):
+        columns = pl.multiple_of(from_y * tile_x, tile_x)
+        if n == SPEED:
+            return vel.at[pl.ds(which * middle, middle), pl.ds(columns, tile_x), :]
+        return field.at[
+            places[n], pl.ds(4 + which * middle, middle), pl.ds(pl.multiple_of(8 + columns, 8), tile_x), :
+        ]
+
+    def half_copy(n, a):
+        return pltpu.make_async_remote_copy(
+            src_ref=sources[n].at[pl.ds(a * n_i + shot * middle, middle)], dst_ref=half_landing(n, y, shot),
+            send_sem=rt_send.at[n, a], recv_sem=rt_recv.at[n, y],
+            device_id={"xline": mate, "inline": lax.rem(a + z_odd, 2)}, device_id_type=MESH,
+        )
+
+    def half_arrival(n):
+        return pltpu.make_async_remote_copy(
+            src_ref=sources[n].at[pl.ds(0, middle)], dst_ref=half_landing(n, 1 - y, shot),
+            send_sem=rt_send.at[n, 0], recv_sem=rt_recv.at[n, 1 - y],
+            device_id={"xline": mate}, device_id_type=MESH,
+        )
+
+    def pass_on(n):
+        return pltpu.make_async_remote_copy(
+            src_ref=half_landing(n, 1 - y, shot), dst_ref=half_landing(n, 1 - y, shot),
+            send_sem=pass_send.at[n], recv_sem=pass_recv.at[n],
+            device_id={"shots": 1 - shot}, device_id_type=MESH,
+        )
+
+    def passed_on(n):
+        return pltpu.make_async_remote_copy(
+            src_ref=half_landing(n, 1 - y, shot), dst_ref=half_landing(n, 1 - y, 1 - shot),
+            send_sem=pass_send.at[n], recv_sem=pass_recv.at[n],
+            device_id={"shots": 1 - shot}, device_id_type=MESH,
+        )
 
     def list_copy(a):
         return pltpu.make_async_remote_copy(
@@ -415,10 +470,9 @@
         def _():
             list_copy(a).start()
 
-    for n in (RHO, NOW):
+    for n in (RHO, SPEED, NOW):
         tile_start(n)
-    for n in (SPEED, BEFORE):
-        tile_start(n)
+    tile_start(BEFORE)
 
     obs_in[me] = observed[...]
 
@@ -499,6 +553,9 @@
                 lap, slope_i, slope_x = lap + terms[0], slope_i + terms[1], slope_x + terms[2]
         return lap, slope_i, slope_x
 
+    for n in shares:
+        half_arrival(n).wait_recv()
+        pass_on(n).start()
     tile_finish(RHO)
     send_all(DENSITY)
     tile_finish(NOW)
@@ -845,6 +902,7 @@
             dma((n_group,)), dma((n_group,)),
             dma((2, 2)), dma((2, 2)), dma((2,)),
             dma((n_xline,)), dma((2, n_xline // 2)), dma((1,)), dma((5,)),
+            dma((6,)), dma((6,)),
         ],
         compiler_params=pltpu.CompilerParams(
             collective_id=0, has_side_effects=True, vmem_limit_bytes=56 * 1024 * 1024

time: 76.6 us -> 74.4 us (0.971); the launches traced: 76.4 us -> 73.1 us
  Pallas kernels: 75.8 us -> 72.5 us
    pallas_call x1, Pallas kernels: 73 us -> 69.8 us  [per_device(): pl.pallas_call(kernel, out_shape=[jax.ShapeDtypeStruct(grad_shape, jnp.fl...]
where the time goes in v5:
time: 74.4 us; the launch traced here: 73.1 us
  Pallas kernels  72.5 us (97%)
    pallas_call x1, Pallas kernels, per_device(): pl.pallas_call(kernel, out_shape=[jax.ShapeDtypeStruct(grad_shape, jnp.fl...  69.8 us
    pallas_call x1, Pallas kernels, finish_kernel(): pl.pallas_call(kernel, out_shape=[jax.ShapeDtypeStruct(dims, jnp.float32)...  2.71 us

profile of v5, /device:TPU:0, one launch (start us, length us, event | category | flops | bytes accessed | tf_op | source)
XLA Modules:
  0.0 73.1 jit_solution(10446916250845656894)
XLA Ops:
  0.6 69.8 %shard_map.130 = (f32[2,4,64,128]{3,2,1,0:T(8,128)}, f32[32,8,256]{2,1,0:T(8,128)}, f32[32,8,256]{2,1,0:T(8,128)}) custom-call(f32[32,8,256]{2,1,0:T(8,128)} %log_density.1, f32[32,8,256]{2,1,0:T(8,128)} %fwd_now.1, f32[32,8,256]{2,1,0:T(8,128)} %velocity.1, f32[32,8,256]{2,1,0:T(8,128)} %fwd_before.1, f32[32,8,256]{2,1,0:T(8,128)} %adj_now.1, ...), custom_call_target="tpu_custom_call" | custom-call | tf_op jit(solution)/shard_map/pallas_call | solution.py:865
  70.4 2.7 %shard_map.131 = (f32[32,32,64]{2,1,0:T(8,128)}, f32[32,8,256]{2,1,0:T(8,128)}, f32[32,8,256]{2,1,0:T(8,128)}) custom-call(f32[2,4,64,128]{3,2,1,0:T(8,128)} %get-tuple-element.6.slabs_in, f32[32,8,256]{2,1,0:T(8,128)} %get-tuple-element.7.last_in, f32[32,8,256]{2,1,0:T(8,128)} %get-tuple-element.8.previous_in), custom_call_target="tpu_custom_call" | custom-call | tf_op jit(solution)/shard_map/pallas_call | solution.py:831

commit v6 on v5

--- a/solution.py
+++ b/solution.py
@@ -55,7 +55,7 @@
     log_density, fwd_now, velocity, fwd_before, adj_now, adj_before,
     given_observed, given_cells, given_counts, given_src, given_wavelet,
     grad_out, last_out, previous_out,
-    field, vel, x_in, x_out, i_in, accel, base, image, slopes, speed_sq, wx,
+    field, vel, x_in, x_out, i_in, i_out, accel, base, image, slopes, speed_sq, wx,
     row_map, zmap_t, z_mat, residual_ref, traces, list_out, list_in, obs_in, g_send,
     held_observed, held_cells, held_counts, held_src, held_wavelet, row_mat, wide, deep,
     x_send, x_recv, i_send, i_recv, rt_send, rt_recv, rt_local, list_send, list_recv, obs_send, obs_recv,
@@ -132,18 +132,16 @@
         part_rows = pl.ds(part * middle, middle)
         return pltpu.make_async_remote_copy(
             src_ref=x_out.at[idx, way, d, part_rows], dst_ref=x_in.at[idx, 1 - way, d, part_rows],
-            send_sem=x_send.at[idx, way, part, d], recv_sem=x_recv.at[idx, way, part, d],
+            send_sem=x_send.at[idx, way], recv_sem=x_recv.at[idx, way, part, d],
             device_id=target[way], device_id_type=MESH,
         )
 
     def above(idx, part, c, d, arriving):
         up = part == 0
         return pltpu.make_async_remote_copy(
-            src_ref=field.at[
-                idx, pl.ds(4 + part * (n_i - 4), 4), pl.ds(8 + c * half_x, half_x), pl.ds(d * 128, 128)
-            ],
+            src_ref=i_out.at[idx, part, d, c],
             dst_ref=i_in.at[idx, part if arriving else 1 - part, d, c],
-            send_sem=i_send.at[idx, part, c, d],
+            send_sem=i_send.at[idx, part],
             recv_sem=i_recv.at[idx, 1 - part if arriving else part, c, d],
             device_id={
                 "xline": jnp.where(up, target[UP]["xline"], target[DOWN]["xline"]), "inline": other_core
@@ -166,19 +164,38 @@
     def finish(idx, part, d, c):
         @pl.when(has[c])
         def _():
-            beside(idx, c, part, d).wait_send()
             beside(idx, 1 - c, part, d).wait_recv()
 
         @pl.when(has_row(part))
         def _():
-            above(idx, part, c, d, False).wait_send()
             above(idx, part, c, d, True).wait_recv()
+
+    def sent(idx):
+        for n in range(2):
+            @pl.when(has[n])
+            def _():
+                pltpu.make_async_remote_copy(
+                    src_ref=x_out.at[idx, n], dst_ref=x_in.at[idx, 1 - n],
+                    send_sem=x_send.at[idx, n], recv_sem=x_recv.at[idx, n, 0, 0],
+                    device_id=target[n], device_id_type=MESH,
+                ).wait_send()
+
+            @pl.when(has[UP + n])
+            def _():
+                pltpu.make_async_remote_copy(
+                    src_ref=i_out.at[idx, n], dst_ref=i_in.at[idx, 1 - n],
+                    send_sem=i_send.at[idx, n], recv_sem=i_recv.at[idx, n, 0, 0],
+                    device_id=target[UP + n], device_id_type=MESH,
+                ).wait_send()
 
     def send_all(idx):
         for part, d, c in pieces:
             rows_at = pl.ds(part * middle, middle)
             x_out[idx, c, d, rows_at] = field[
                 idx, pl.ds(4 + part * middle, middle), pl.ds(8 + c * (n_x - 4), 4), pl.ds(d * 128, 128)
+            ]
+            i_out[idx, part, d, c] = field[
+                idx, pl.ds(4 + part * (n_i - 4), 4), pl.ds(8 + c * half_x, half_x), pl.ds(d * 128, 128)
             ]
             send(idx, part, d, c)
 
@@ -257,6 +274,22 @@
                     half_copy(n, a).wait_send()
             pass_on(n).wait_send()
             passed_on(n).wait_recv()
+
+    def quarter_start(n, which):
+        for a in range(2):
+            @pl.when(leaves(a))
+            def _():
+                pltpu.make_async_remote_copy(
+                    src_ref=sources[n].at[pl.ds(a * n_i + which * middle, middle)], dst_ref=half_landing(n, y, which),
+                    send_sem=rt_send.at[n, a], recv_sem=rt_recv.at[n, y],
+                    device_id={"xline": 2 * plane + core, "inline": lax.rem(a + z_odd, 2)},
+                    device_id_type=MESH,
+                ).start()
+
+        if which == 0:
+            @pl.when(stays)
+            def _():
+                own_copy(n).start()
 
     def half_landing(n, from_y, which):
         columns = pl.multiple_of(from_y * tile_x, tile_x)
@@ -439,11 +472,6 @@
             def _():
                 slab_copy(d).wait_send()
 
-    for idx in range(5):
-        field[idx, pl.ds(0, 4)] = jnp.zeros((4,) + field.shape[2:], jnp.float32)
-        field[idx, pl.ds(n_i + 4, 4)] = jnp.zeros((4,) + field.shape[2:], jnp.float32)
-        field[idx, inner_i, pl.ds(0, 8)] = jnp.zeros((n_i, 8, depth), jnp.float32)
-        field[idx, inner_i, pl.ds(8 + n_x, 8)] = jnp.zeros((n_i, 8, depth), jnp.float32)
     for way in (LEFT, RIGHT, UP, DOWN):
         @pl.when(jnp.logical_not(has[way]))
         def _():
@@ -574,6 +602,7 @@
 
     for part, d, c in pieces:
         finish(DENSITY, part, d, c)
+    sent(DENSITY)
     for d in range(layers):
         lanes = pl.ds(d * 128, 128)
         for side in range(2):
@@ -684,6 +713,8 @@
             fresh = field[spot] + change
             field[spot] = fresh
             x_out[other, c, d, i] = fresh[half_x - 4:] if c else fresh[:4]
+            if r < 4:
+                i_out[other, part, d, c, jnp.where(up, r, 3 - r)] = fresh
             if t is not None:
                 accel[t, i, columns, lanes] += change
 
@@ -693,25 +724,29 @@
         predicted = jnp.sum(picked * row_map[...], axis=0, keepdims=True)
         residual_ref[t] = predicted
 
-    def task_now():
-        tile_start(ADJ_NOW)
+    def task_first():
+        quarter_start(ADJ_NOW, 0)
         make_maps()
 
-    def task_before():
-        tile_start(ADJ_BEFORE)
-
-    def task_traces():
+    def task_second():
+        quarter_start(ADJ_NOW, 1)
+
+    def task_third():
+        quarter_start(ADJ_BEFORE, 0)
+
         @pl.loop(1, n_group)
         def _(r):
             obs_copy(lax.rem(me + r, n_group), me).start()
 
     def task_halos():
+        quarter_start(ADJ_BEFORE, 1)
         tile_finish(ADJ_NOW)
         send_all(2)
 
     def task_adjoint():
         tile_finish(ADJ_BEFORE)
         differences(2)
+        vel[...] = (2.0 / steps) / vel[...]
 
         @pl.loop(0, n_i, unroll=2)
         def _(i):
@@ -720,7 +755,7 @@
                 2.0 * center - field[3, i + 4, inner_x, :] + speed_sq[i] * value
             )
 
-    tasks = [task_now, task_before, task_traces, task_halos, task_adjoint, make_traces]
+    tasks = [task_first, task_second, task_third, task_halos, task_adjoint, make_traces]
     times = [1 + n * (steps - 2) // len(tasks) for n in range(len(tasks))]
 
     @pl.loop(0, steps)
@@ -743,6 +778,7 @@
         @pl.when(t >= 1)
         def _():
             sample(now, t - 1)
+            sent(other)
 
         for part, d, c in pieces:
             finish(now, part, d, c)
@@ -752,6 +788,7 @@
             def _():
                 send(other, part, d, c)
 
+    sent((steps - 1) % 2)
     sample(steps % 2, steps - 1)
 
     @pl.loop(0, steps)
@@ -775,6 +812,8 @@
                 center, _ = interior(now, other, i)
                 image[i] += center * accel[t + 1, i]
 
+            sent(other)
+
         @pl.when(j == steps - 1)
         def _():
             home_start(0)
@@ -787,10 +826,11 @@
             def _():
                 send(other, part, d, c)
 
-    @pl.loop(0, n_i)
+    sent(2 + (steps - 1) % 2)
+
+    @pl.loop(0, n_i, unroll=4)
     def _(i):
-        total = image[i] + field[final_idx[1], i + 4, inner_x, :] * accel[0, i]
-        image[i] = total * (2.0 / steps) / vel[i]
+        image[i] = (image[i] + field[final_idx[1], i + 4, inner_x, :] * accel[0, i]) * vel[i]
 
     if fused:
         fused_gradient()
@@ -806,34 +846,54 @@
     _, n_groups, _, lanes = slabs.shape
     group = lanes // dz
 
-    def kernel(slabs_in, last_in, previous_in, gradient, last_out, previous_out, sem):
-        copies = [
-            pltpu.make_async_copy(last_in, last_out, sem.at[0]),
-            pltpu.make_async_copy(previous_in, previous_out, sem.at[1]),
+    def kernel(
+        slabs_in, last_in, previous_in, gradient, last_out, previous_out,
+        slabs_held, last_held, previous_held, lines_held, in_sem, out_sem,
+    ):
+        loads = [
+            pltpu.make_async_copy(slabs_in, slabs_held, in_sem.at[0]),
+            pltpu.make_async_copy(last_in, last_held, in_sem.at[1]),
+            pltpu.make_async_copy(previous_in, previous_held, in_sem.at[2]),
         ]
-        for copy in copies:
-            copy.start()
+        for load in loads:
+            load.start()
         far = (
             lax.broadcasted_iota(jnp.int32, (full_x, full_x), 0) - lax.broadcasted_iota(jnp.int32, (full_x, full_x), 1)
         ).astype(jnp.float32)
         weights = jnp.exp(-jnp.abs(far) / SMOOTH)
         weights = weights / jnp.sum(weights, axis=0, keepdims=True)
+        stores = [
+            pltpu.make_async_copy(last_held, last_out, out_sem.at[0]),
+            pltpu.make_async_copy(previous_held, previous_out, out_sem.at[1]),
+        ]
+        for load, store in zip(loads[1:], stores):
+            load.wait()
+            store.start()
+        loads[0].wait()
         for a in range(2):
             for ig in range(n_groups):
-                lines = dot_tn_exact(slabs_in[a, ig], weights)
+                lines = dot_tn_exact(slabs_held[a, ig], weights)
                 for j in range(group):
-                    gradient[:, (a * n_groups + ig) * group + j, :] = lines[j * dz:(j + 1) * dz]
-        for copy in copies:
-            copy.wait()
-
-    vmem = pl.BlockSpec(memory_space=pltpu.VMEM)
+                    lines_held[:, (a * n_groups + ig) * group + j, :] = lines[j * dz:(j + 1) * dz]
+            span = pl.ds(a * (tile_i // 2), tile_i // 2)
+            store = pltpu.make_async_copy(lines_held.at[:, span, :], gradient.at[:, span, :], out_sem.at[2 + a])
+            store.start()
+            stores.append(store)
+        for store in stores:
+            store.wait()
+
     anywhere = pl.BlockSpec(memory_space=pl.ANY)
     return pl.pallas_call(
         kernel,
         out_shape=[jax.ShapeDtypeStruct(dims, jnp.float32) for dims in (shape, last.shape, previous.shape)],
-        in_specs=[vmem] * 3,
-        out_specs=[vmem, anywhere, anywhere],
-        scratch_shapes=[pltpu.SemaphoreType.DMA((2,))],
+        in_specs=[anywhere] * 3,
+        out_specs=[anywhere] * 3,
+        scratch_shapes=[
+            *[pltpu.VMEM(dims, jnp.float32) for dims in (slabs.shape, last.shape, previous.shape, shape)],
+            pltpu.SemaphoreType.DMA((3,)),
+            pltpu.SemaphoreType.DMA((4,)),
+        ],
+        compiler_params=pltpu.CompilerParams(vmem_limit_bytes=56 * 1024 * 1024),
     )(slabs, last, previous)
 
 
@@ -877,6 +937,7 @@
             pltpu.VMEM((5, 2, layers, n_i, 4, 128), jnp.float32),
             pltpu.VMEM((5, 2, layers, n_i, 4, 128), jnp.float32),
             pltpu.VMEM((5, 2, layers, 2, 4, tile_x, 128), jnp.float32),
+            pltpu.VMEM((5, 2, layers, 2, 4, tile_x, 128), jnp.float32),
             pltpu.VMEM((steps,) + block, jnp.float32),
             pltpu.VMEM(block, jnp.float32),
             pltpu.VMEM(block, jnp.float32),
@@ -896,7 +957,7 @@
             pltpu.VMEM((3 * rows, rows), jnp.bfloat16),
             pltpu.VMEM((3 * rows, depth), jnp.float32),
             pltpu.VMEM((rows, 2 * depth), jnp.float32),
-            *[dma((5, 2, 2, layers)) for _ in range(4)],
+            dma((5, 2)), dma((5, 2, 2, layers)), dma((5, 2)), dma((5, 2, 2, layers)),
             dma((6, 2)), dma((6, 2)), dma((6,)),
             dma((2,)), dma((2,)),
             dma((n_group,)), dma((n_group,)),

time: 74.4 us -> 73.5 us (0.988)
  no operation moved by 1% of the time
where the time goes in v6:
time: 73.5 us; the launch traced here: 72.4 us
  Pallas kernels  71.8 us (98%)
    pallas_call x1, Pallas kernels, per_device(): pl.pallas_call(kernel, out_shape=[jax.ShapeDtypeStruct(grad_shape, jnp.fl...  69.3 us
    pallas_call x1, Pallas kernels, finish_kernel(): pl.pallas_call(kernel, out_shape=[jax.ShapeDtypeStruct(dims, jnp.float32)...  2.45 us

profile of v6, /device:TPU:0, one launch (start us, length us, event | category | flops | bytes accessed | tf_op | source)
XLA Modules:
  0.0 72.4 jit_solution(14966398433885860894)
XLA Ops:
  0.6 69.3 %shard_map.130 = (f32[2,4,64,128]{3,2,1,0:T(8,128)}, f32[32,8,256]{2,1,0:T(8,128)}, f32[32,8,256]{2,1,0:T(8,128)}) custom-call(f32[32,8,256]{2,1,0:T(8,128)} %log_density.1, f32[32,8,256]{2,1,0:T(8,128)} %fwd_now.1, f32[32,8,256]{2,1,0:T(8,128)} %velocity.1, f32[32,8,256]{2,1,0:T(8,128)} %fwd_before.1, f32[32,8,256]{2,1,0:T(8,128)} %adj_now.1, ...), custom_call_target="tpu_custom_call" | custom-call | tf_op jit(solution)/shard_map/pallas_call | solution.py:925
  70.0 2.4 %shard_map.131 = (f32[32,32,64]{2,1,0:T(8,128)}, f32[32,8,256]{2,1,0:T(8,128)}, f32[32,8,256]{2,1,0:T(8,128)}) custom-call(f32[2,4,64,128]{3,2,1,0:T(8,128)} %get-tuple-element.6.slabs_in, f32[32,8,256]{2,1,0:T(8,128)} %get-tuple-element.7.last_in, f32[32,8,256]{2,1,0:T(8,128)} %get-tuple-element.8.previous_in), custom_call_target="tpu_custom_call" | custom-call | tf_op jit(solution)/shard_map/pallas_call | solution.py:886

commit v7 on v6

--- a/solution.py
+++ b/solution.py
@@ -600,6 +600,25 @@
 
     accel[0] = inject_sources(0).reshape(n_i, n_x, depth)
 
+    for from_y in range(2):
+        @pl.when(arrives(from_y))
+        def _():
+            list_arrival(from_y).wait_recv()
+    for a in range(2):
+        @pl.when(leaves(a))
+        def _():
+            list_copy(a).wait_send()
+    for from_y in range(2):
+        spot = list_in[from_y][:1]
+        cell_i = div(spot, tile_x * depth) - cp * n_i
+        cell_x = mod(div(spot, depth), tile_x) + from_y * tile_x
+        row = jnp.where((spot >= 0) & (cell_i >= 0) & (cell_i < n_i), cell_i * n_x + cell_x, -1)
+        columns = pl.ds(from_y * slots, slots)
+        row_map[:, columns] = (lax.broadcasted_iota(jnp.int32, (rows, slots), 0) == row).astype(jnp.float32)
+        zmap_t[:, columns] = (
+            lax.broadcasted_iota(jnp.int32, (depth, slots), 0) == mod(spot, depth)
+        ).astype(jnp.float32).astype(jnp.bfloat16)
+
     for part, d, c in pieces:
         finish(DENSITY, part, d, c)
     sent(DENSITY)
@@ -641,44 +660,30 @@
             2.0 * field[0, i + 4, inner_x, :] - field[1, i + 4, inner_x, :] + accel[0, i]
         )
 
-    def make_maps():
-        for from_y in range(2):
-            @pl.when(arrives(from_y))
-            def _():
-                list_arrival(from_y).wait_recv()
-        for a in range(2):
-            @pl.when(leaves(a))
-            def _():
-                list_copy(a).wait_send()
-        for from_y in range(2):
-            spot = list_in[from_y][:1]
-            cell_i = div(spot, tile_x * depth) - cp * n_i
-            cell_x = mod(div(spot, depth), tile_x) + from_y * tile_x
-            row = jnp.where((spot >= 0) & (cell_i >= 0) & (cell_i < n_i), cell_i * n_x + cell_x, -1)
-            columns = pl.ds(from_y * slots, slots)
-            row_map[:, columns] = (lax.broadcasted_iota(jnp.int32, (rows, slots), 0) == row).astype(jnp.float32)
-            zmap_t[:, columns] = (
-                lax.broadcasted_iota(jnp.int32, (depth, slots), 0) == mod(spot, depth)
-            ).astype(jnp.float32).astype(jnp.bfloat16)
-
-    def make_traces():
+    def start_traces(third):
+        @pl.loop(1 + (n_group - 1) * third // 3, 1 + (n_group - 1) * (third + 1) // 3)
+        def _(r):
+            obs_copy(lax.rem(me + r, n_group), me).start()
+
+    def make_traces(from_y):
         @pl.loop(1, n_group)
         def _(r):
             peer = lax.rem(me + r, n_group)
-            obs_copy(peer, peer).wait_recv()
-            obs_copy(peer, me).wait_send()
+            if from_y == 0:
+                obs_copy(peer, peer).wait_recv()
+            else:
+                obs_copy(peer, me).wait_send()
 
         lane = div(lax.broadcasted_iota(jnp.int32, (8, slots), 1), CAP)
-        for from_y in range(2):
-            owner = (2 * plane + from_y) * 2 + origin
-
-            def place_one(s, total):
-                moved = pltpu.roll(obs_in[s], lax.rem(s - owner + n_group, n_group) * CAP, axis=1)
-                return jnp.where(lane == s, moved, total)
-
-            traces[:, pl.ds(from_y * slots, slots)] = lax.fori_loop(
-                0, n_group, place_one, jnp.zeros((8, slots), jnp.float32)
-            )
+        owner = (2 * plane + from_y) * 2 + origin
+
+        def place_one(s, total):
+            moved = pltpu.roll(obs_in[s], lax.rem(s - owner + n_group, n_group) * CAP, axis=1)
+            return jnp.where(lane == s, moved, total)
+
+        traces[:, pl.ds(from_y * slots, slots)] = lax.fori_loop(
+            0, n_group, place_one, jnp.zeros((8, slots), jnp.float32)
+        )
 
     def prepare(idx, term):
         base[...] = term.reshape(n_i, n_x, depth)
@@ -726,20 +731,17 @@
 
     def task_first():
         quarter_start(ADJ_NOW, 0)
-        make_maps()
 
     def task_second():
         quarter_start(ADJ_NOW, 1)
 
     def task_third():
         quarter_start(ADJ_BEFORE, 0)
-
-        @pl.loop(1, n_group)
-        def _(r):
-            obs_copy(lax.rem(me + r, n_group), me).start()
+        start_traces(0)
 
     def task_halos():
         quarter_start(ADJ_BEFORE, 1)
+        start_traces(1)
         tile_finish(ADJ_NOW)
         send_all(2)
 
@@ -747,6 +749,7 @@
         tile_finish(ADJ_BEFORE)
         differences(2)
         vel[...] = (2.0 / steps) / vel[...]
+        start_traces(2)
 
         @pl.loop(0, n_i, unroll=2)
         def _(i):
@@ -755,8 +758,9 @@
                 2.0 * center - field[3, i + 4, inner_x, :] + speed_sq[i] * value
             )
 
-    tasks = [task_first, task_second, task_third, task_halos, task_adjoint, make_traces]
-    times = [1 + n * (steps - 2) // len(tasks) for n in range(len(tasks))]
+    tasks = [task_first, task_second, task_third, task_halos, task_adjoint]
+    tasks += [functools.partial(make_traces, 0), functools.partial(make_traces, 1)]
+    times = [1 + n * (steps - 1) // len(tasks) for n in range(len(tasks))]
 
     @pl.loop(0, steps)
     def _(t):

time: 73.5 us -> 73.6 us (level)
  no operation moved by 1% of the time
where the time goes in v7:
time: 73.6 us; the launch traced here: 72.2 us
  Pallas kernels  71.5 us (97%)
    pallas_call x1, Pallas kernels, per_device(): pl.pallas_call(kernel, out_shape=[jax.ShapeDtypeStruct(grad_shape, jnp.fl...  69.1 us
    pallas_call x1, Pallas kernels, finish_kernel(): pl.pallas_call(kernel, out_shape=[jax.ShapeDtypeStruct(dims, jnp.float32)...  2.45 us

profile of v7, /device:TPU:0, one launch (start us, length us, event | category | flops | bytes accessed | tf_op | source)
XLA Modules:
  0.0 72.2 jit_solution(7157922847705966114)
XLA Ops:
  0.6 69.1 %shard_map.130 = (f32[2,4,64,128]{3,2,1,0:T(8,128)}, f32[32,8,256]{2,1,0:T(8,128)}, f32[32,8,256]{2,1,0:T(8,128)}) custom-call(f32[32,8,256]{2,1,0:T(8,128)} %log_density.1, f32[32,8,256]{2,1,0:T(8,128)} %fwd_now.1, f32[32,8,256]{2,1,0:T(8,128)} %velocity.1, f32[32,8,256]{2,1,0:T(8,128)} %fwd_before.1, f32[32,8,256]{2,1,0:T(8,128)} %adj_now.1, ...), custom_call_target="tpu_custom_call" | custom-call | tf_op jit(solution)/shard_map/pallas_call | solution.py:929
  69.7 2.4 %shard_map.131 = (f32[32,32,64]{2,1,0:T(8,128)}, f32[32,8,256]{2,1,0:T(8,128)}, f32[32,8,256]{2,1,0:T(8,128)}) custom-call(f32[2,4,64,128]{3,2,1,0:T(8,128)} %get-tuple-element.6.slabs_in, f32[32,8,256]{2,1,0:T(8,128)} %get-tuple-element.7.last_in, f32[32,8,256]{2,1,0:T(8,128)} %get-tuple-element.8.previous_in), custom_call_target="tpu_custom_call" | custom-call | tf_op jit(solution)/shard_map/pallas_call | solution.py:890

commit v8 on v7

--- a/solution.py
+++ b/solution.py
@@ -737,11 +737,14 @@
 
     def task_third():
         quarter_start(ADJ_BEFORE, 0)
+
+    def task_fourth():
+        quarter_start(ADJ_BEFORE, 1)
         start_traces(0)
+        start_traces(1)
 
     def task_halos():
-        quarter_start(ADJ_BEFORE, 1)
-        start_traces(1)
+        start_traces(2)
         tile_finish(ADJ_NOW)
         send_all(2)
 
@@ -749,7 +752,6 @@
         tile_finish(ADJ_BEFORE)
         differences(2)
         vel[...] = (2.0 / steps) / vel[...]
-        start_traces(2)
 
         @pl.loop(0, n_i, unroll=2)
         def _(i):
@@ -758,9 +760,8 @@
                 2.0 * center - field[3, i + 4, inner_x, :] + speed_sq[i] * value
             )
 
-    tasks = [task_first, task_second, task_third, task_halos, task_adjoint]
-    tasks += [functools.partial(make_traces, 0), functools.partial(make_traces, 1)]
-    times = [1 + n * (steps - 1) // len(tasks) for n in range(len(tasks))]
+    tasks = [task_first, task_second, task_third, task_fourth, task_halos, functools.partial(make_traces, 0), functools.partial(make_traces, 1), task_adjoint]
+    times = [n * steps // 8 for n in (0, 1, 2, 3, 4, 6, 7, 5)]
 
     @pl.loop(0, steps)
     def _(t):

time: 73.6 us -> 72 us (0.978)
  Pallas kernels: 71.5 us -> 70 us
    pallas_call x1, Pallas kernels: 69.1 us -> 67.5 us  [per_device(): pl.pallas_call(kernel, out_shape=[jax.ShapeDtypeStruct(grad_shape, jnp.fl...]
where the time goes in v8:
time: 72 us; the launch traced here: 70.6 us
  Pallas kernels  70 us (97%)
    pallas_call x1, Pallas kernels, per_device(): pl.pallas_call(kernel, out_shape=[jax.ShapeDtypeStruct(grad_shape, jnp.fl...  67.5 us
    pallas_call x1, Pallas kernels, finish_kernel(): pl.pallas_call(kernel, out_shape=[jax.ShapeDtypeStruct(dims, jnp.float32)...  2.44 us

profile of v8, /device:TPU:0, one launch (start us, length us, event | category | flops | bytes accessed | tf_op | source)
XLA Modules:
  0.0 70.6 jit_solution(14731732982674184640)
XLA Ops:
  0.6 67.5 %shard_map.130 = (f32[2,4,64,128]{3,2,1,0:T(8,128)}, f32[32,8,256]{2,1,0:T(8,128)}, f32[32,8,256]{2,1,0:T(8,128)}) custom-call(f32[32,8,256]{2,1,0:T(8,128)} %log_density.1, f32[32,8,256]{2,1,0:T(8,128)} %fwd_now.1, f32[32,8,256]{2,1,0:T(8,128)} %velocity.1, f32[32,8,256]{2,1,0:T(8,128)} %fwd_before.1, f32[32,8,256]{2,1,0:T(8,128)} %adj_now.1, ...), custom_call_target="tpu_custom_call" | custom-call | tf_op jit(solution)/shard_map/pallas_call | solution.py:930
  68.2 2.4 %shard_map.131 = (f32[32,32,64]{2,1,0:T(8,128)}, f32[32,8,256]{2,1,0:T(8,128)}, f32[32,8,256]{2,1,0:T(8,128)}) custom-call(f32[2,4,64,128]{3,2,1,0:T(8,128)} %get-tuple-element.6.slabs_in, f32[32,8,256]{2,1,0:T(8,128)} %get-tuple-element.7.last_in, f32[32,8,256]{2,1,0:T(8,128)} %get-tuple-element.8.previous_in), custom_call_target="tpu_custom_call" | custom-call | tf_op jit(solution)/shard_map/pallas_call | solution.py:891

commit v9 on v8

--- a/solution.py
+++ b/solution.py
@@ -56,7 +56,7 @@
     given_observed, given_cells, given_counts, given_src, given_wavelet,
     grad_out, last_out, previous_out,
     field, vel, x_in, x_out, i_in, i_out, accel, base, image, slopes, speed_sq, wx,
-    row_map, zmap_t, z_mat, residual_ref, traces, list_out, list_in, obs_in, g_send,
+    row_map, zmap_t, zmap, z_mat, residual_ref, traces, list_out, list_in, obs_in, g_send,
     held_observed, held_cells, held_counts, held_src, held_wavelet, row_mat, wide, deep,
     x_send, x_recv, i_send, i_recv, rt_send, rt_recv, rt_local, list_send, list_recv, obs_send, obs_recv,
     ret_send, ret_recv, ret_local, g_ssem, g_rsem, g_local, small_sem, pass_send, pass_recv,
@@ -619,6 +619,8 @@
             lax.broadcasted_iota(jnp.int32, (depth, slots), 0) == mod(spot, depth)
         ).astype(jnp.float32).astype(jnp.bfloat16)
 
+    zmap[...] = zmap_t[...].astype(jnp.float32).T.astype(jnp.bfloat16)
+
     for part, d, c in pieces:
         finish(DENSITY, part, d, c)
     sent(DENSITY)
@@ -742,9 +744,9 @@
         quarter_start(ADJ_BEFORE, 1)
         start_traces(0)
         start_traces(1)
+        start_traces(2)
 
     def task_halos():
-        start_traces(2)
         tile_finish(ADJ_NOW)
         send_all(2)
 
@@ -772,7 +774,7 @@
         def _():
             prepare(now, inject_sources(t))
 
-            @pl.loop(0, n_i, unroll=2)
+            @pl.loop(0, n_i, unroll=8)
             def _(i):
                 _, change = interior(now, other, i)
                 accel[t, i] = change
@@ -802,7 +804,7 @@
         other = 5 - now
         t = steps - 1 - j
         high, low = split_bf16(row_map[...] * (residual_ref[t] - traces[pl.ds(t, 1), :]))
-        injected = dot_nt(high, zmap_t[...]) + dot_nt(low, zmap_t[...])
+        injected = dot(high, zmap[...]) + dot(low, zmap[...])
 
         @pl.when(j == 0)
         def _():
@@ -812,7 +814,7 @@
         def _():
             prepare(now, injected)
 
-            @pl.loop(0, n_i, unroll=2)
+            @pl.loop(0, n_i, unroll=8)
             def _(i):
                 center, _ = interior(now, other, i)
                 image[i] += center * accel[t + 1, i]
@@ -951,6 +953,7 @@
             pltpu.VMEM((4,) + block, jnp.float32),
             pltpu.VMEM((rows, 2 * slots), jnp.float32),
             pltpu.VMEM((depth, 2 * slots), jnp.bfloat16),
+            pltpu.VMEM((2 * slots, depth), jnp.bfloat16),
             pltpu.VMEM((depth, 2 * depth), jnp.bfloat16),
             pltpu.VMEM((steps, 1, 2 * slots), jnp.float32),
             pltpu.VMEM((steps, 2 * slots), jnp.float32),

time: 72 us -> 71.3 us (level); the launches traced: 70.6 us -> 70.7 us
  no operation moved by 1% of the time
where the time goes in v9:
time: 71.3 us; the launch traced here: 70.7 us
  Pallas kernels  70.1 us (98%)
    pallas_call x1, Pallas kernels, per_device(): pl.pallas_call(kernel, out_shape=[jax.ShapeDtypeStruct(grad_shape, jnp.fl...  67.6 us
    pallas_call x1, Pallas kernels, finish_kernel(): pl.pallas_call(kernel, out_shape=[jax.ShapeDtypeStruct(dims, jnp.float32)...  2.45 us

profile of v9, /device:TPU:0, one launch (start us, length us, event | category | flops | bytes accessed | tf_op | source)
XLA Modules:
  0.0 70.7 jit_solution(12524038349180776653)
XLA Ops:
  0.6 67.6 %shard_map.130 = (f32[2,4,64,128]{3,2,1,0:T(8,128)}, f32[32,8,256]{2,1,0:T(8,128)}, f32[32,8,256]{2,1,0:T(8,128)}) custom-call(f32[32,8,256]{2,1,0:T(8,128)} %log_density.1, f32[32,8,256]{2,1,0:T(8,128)} %fwd_now.1, f32[32,8,256]{2,1,0:T(8,128)} %velocity.1, f32[32,8,256]{2,1,0:T(8,128)} %fwd_before.1, f32[32,8,256]{2,1,0:T(8,128)} %adj_now.1, ...), custom_call_target="tpu_custom_call" | custom-call | tf_op jit(solution)/shard_map/pallas_call | solution.py:932
  68.3 2.4 %shard_map.131 = (f32[32,32,64]{2,1,0:T(8,128)}, f32[32,8,256]{2,1,0:T(8,128)}, f32[32,8,256]{2,1,0:T(8,128)}) custom-call(f32[2,4,64,128]{3,2,1,0:T(8,128)} %get-tuple-element.6.slabs_in, f32[32,8,256]{2,1,0:T(8,128)} %get-tuple-element.7.last_in, f32[32,8,256]{2,1,0:T(8,128)} %get-tuple-element.8.previous_in), custom_call_target="tpu_custom_call" | custom-call | tf_op jit(solution)/shard_map/pallas_call | solution.py:893

commit v10 on v9

--- a/solution.py
+++ b/solution.py
@@ -755,7 +755,7 @@
         differences(2)
         vel[...] = (2.0 / steps) / vel[...]
 
-        @pl.loop(0, n_i, unroll=2)
+        @pl.loop(0, n_i, unroll=8)
         def _(i):
             center, value = operator(2, i)
             field[3, i + 4, inner_x, :] = (
@@ -774,7 +774,7 @@
         def _():
             prepare(now, inject_sources(t))
 
-            @pl.loop(0, n_i, unroll=8)
+            @pl.loop(0, n_i, unroll=16)
             def _(i):
                 _, change = interior(now, other, i)
                 accel[t, i] = change
@@ -814,7 +814,7 @@
         def _():
             prepare(now, injected)
 
-            @pl.loop(0, n_i, unroll=8)
+            @pl.loop(0, n_i, unroll=16)
             def _(i):
                 center, _ = interior(now, other, i)
                 image[i] += center * accel[t + 1, i]
@@ -835,7 +835,7 @@
 
     sent(2 + (steps - 1) % 2)
 
-    @pl.loop(0, n_i, unroll=4)
+    @pl.loop(0, n_i, unroll=16)
     def _(i):
         image[i] = (image[i] + field[final_idx[1], i + 4, inner_x, :] * accel[0, i]) * vel[i]
 

time: 71.3 us -> 70.9 us (level)
  Pallas kernels: 70.1 us -> 69 us
    pallas_call x1, Pallas kernels: 67.6 us -> 66.5 us  [per_device(): pl.pallas_call(kernel, out_shape=[jax.ShapeDtypeStruct(grad_shape, jnp.fl...]
where the time goes in v10:
time: 70.9 us; the launch traced here: 69.6 us
  Pallas kernels  69 us (97%)
    pallas_call x1, Pallas kernels, per_device(): pl.pallas_call(kernel, out_shape=[jax.ShapeDtypeStruct(grad_shape, jnp.fl...  66.5 us
    pallas_call x1, Pallas kernels, finish_kernel(): pl.pallas_call(kernel, out_shape=[jax.ShapeDtypeStruct(dims, jnp.float32)...  2.44 us

profile of v10, /device:TPU:0, one launch (start us, length us, event | category | flops | bytes accessed | tf_op | source)
XLA Modules:
  0.0 69.6 jit_solution(16124522816163018862)
XLA Ops:
  0.6 66.5 %shard_map.130 = (f32[2,4,64,128]{3,2,1,0:T(8,128)}, f32[32,8,256]{2,1,0:T(8,128)}, f32[32,8,256]{2,1,0:T(8,128)}) custom-call(f32[32,8,256]{2,1,0:T(8,128)} %log_density.1, f32[32,8,256]{2,1,0:T(8,128)} %fwd_now.1, f32[32,8,256]{2,1,0:T(8,128)} %velocity.1, f32[32,8,256]{2,1,0:T(8,128)} %fwd_before.1, f32[32,8,256]{2,1,0:T(8,128)} %adj_now.1, ...), custom_call_target="tpu_custom_call" | custom-call | tf_op jit(solution)/shard_map/pallas_call | solution.py:932
  67.2 2.4 %shard_map.131 = (f32[32,32,64]{2,1,0:T(8,128)}, f32[32,8,256]{2,1,0:T(8,128)}, f32[32,8,256]{2,1,0:T(8,128)}) custom-call(f32[2,4,64,128]{3,2,1,0:T(8,128)} %get-tuple-element.6.slabs_in, f32[32,8,256]{2,1,0:T(8,128)} %get-tuple-element.7.last_in, f32[32,8,256]{2,1,0:T(8,128)} %get-tuple-element.8.previous_in), custom_call_target="tpu_custom_call" | custom-call | tf_op jit(solution)/shard_map/pallas_call | solution.py:893
